TPU v7x, 32 devices: a whole 2x2x4 slice. The times are simulated.
32 devices in a mesh: dp: 4 (over y, x), ctx: 8 (over z, core).
Axes of the slice: x: 2, y: 2, z: 4, core: 2. Of those that a mesh axis runs over, the one named last changes fastest.
Arguments:
- inputs: bfloat16 [8192, 8192], P(('dp', 'ctx')), parts along dimension 0, may hold values from -6 to 6
- key_query: bfloat16 [8192, 2048], P(('dp', 'ctx')), parts along dimension 0, may hold values from -3 to 3
- conv_inputs: float32 [4, 8192], replicated, may hold values from -3 to 3
- conv_kq: float32 [4, 2048], replicated, may hold values from -3 to 3
- step_size: float32 [8192, 128], P(('dp', 'ctx')), parts along dimension 0, may hold values from 0.1 to 1
- decay_log: float32 [8192, 128], P(('dp', 'ctx')), parts along dimension 0, may hold values from -1 to 0, as said below
- skip_gain: float32 [128], replicated, may hold values from 0.5 to 1.5
- norm_gain: float32 [8192], replicated, may hold values from 0.5 to 1.5
Outputs:
- mixed: bfloat16 [8192, 8192], P('dp', 'ctx'), parts along dimension 0
There are 4 independent parts, one for each index of `dp`. A program takes and returns all parts, laid end to end along the dimension named above; an argument that names none is the same for every part. Nothing has to cross between parts.
Inputs may be any that keep to these rules, and one draw needn't show every extreme that they name: `decay_log`: log decay factors, all negative.
All inputs are finite; a program needn't handle non-finite values.
Results may differ from a plain program's by a relative error of at most 0.0085.
Values may be sent and summed in bfloat16 or wider, within the bound.
No kernel may reach another device: no remote copies, remote signals or barrier semaphores. Data moves between devices by JAX's collectives and lax.ppermute only.
A program may use at most 448 MiB of HBM per device.

v0:
```python
import functools
import math

import jax
import jax.numpy as jnp
from jax import lax
from jax.experimental import pallas as pl
from jax.experimental.pallas import tpu as pltpu
from jax.sharding import PartitionSpec as P

HEADS = 128
HEAD_DIM = 64
STATE = 128
GROUPS = 8
KW = 4
BLOCK = 128
GROUP_WIDTH = HEADS * HEAD_DIM // GROUPS
EPS = 1e-05
HALO = 16
LANES = 128
FIELDS = 3
STRIP = 64
PACK_VMEM = 58 * 1024 * 1024
VMEM_LIMIT = 32 * 1024 * 1024


def contract(a, b, dims):
    return lax.dot_general(a, b, (dims, ((), ())), preferred_element_type=jnp.float32)


def as_parts(v, count):
    parts = []
    for _ in range(count):
        part = v.astype(jnp.bfloat16)
        parts.append(part)
        v = v - part.astype(jnp.float32)
    return parts


def relative(me, ring, code):
    place = lax.rem(me // 2 + code // 2, ring)
    return 2 * place + ((me & 1) ^ (code & 1))


def pack_kernel(peers, span, widths, heads, entries, scalar_rows, *refs):
    refs = list(refs)
    me = refs.pop(0)[0]
    x_ref = refs.pop(0)
    heading = scalar_rows > 0
    if heading:
        kq_ref, decay_ref, step_ref = refs[:3]
        del refs[:3]
    outs = refs[: len(entries)]
    del refs[: len(entries)]
    if heading:
        raw_scalars, scalars, kq_near = refs[:3]
    sems = refs[-1]
    rows = x_ref.shape[0]
    owned = HEADS * HEAD_DIM // peers
    lead = widths[0] + 2 * STATE
    copies = []
    if heading:
        loads = [
            pltpu.make_async_copy(ref, raw_scalars.at[i], sems.at[2, i])
            for i, ref in enumerate((decay_ref, step_ref))
        ]
        loads.append(pltpu.make_async_copy(kq_ref, kq_near, sems.at[2, 2]))
        for load in loads:
            load.start()
    owners = [relative(me, peers // 2, code) for code, _ in entries]
    for i, (owner, (_, kind)) in enumerate(zip(owners, entries)):
        pieces = {
            "full": [(0, 0, 0), (1, widths[0], lead)],
            "lead": [(0, 0, 0)],
            "rest": [(1, widths[0], 0)],
        }[kind]
        for index, offset, left in pieces:
            column = pl.multiple_of(owner * owned + offset, LANES)
            copies.append(
                pltpu.make_async_copy(
                    x_ref.at[:, pl.ds(column, widths[index])],
                    outs[i].at[0:rows, left : left + widths[index]],
                    sems.at[index, i],
                )
            )
    for copy in copies:
        copy.start()
    if heading:
        for load in loads:
            load.wait()
        fields = as_parts(raw_scalars[0].T, 2) + as_parts(raw_scalars[1].T, 1)
        for p, field in enumerate(fields):
            field = field.astype(jnp.float32)
            for owner in range(peers):
                scalars[p, owner] = field[owner * heads : (owner + 1) * heads]
        across = lead // rows
        for i, owner in enumerate(owners):
            outs[i][rows:] = jnp.zeros((scalar_rows, outs[i].shape[1]), jnp.bfloat16)
            for p in range(FIELDS):
                top = rows + p // across * heads
                left = p % across * rows
                outs[i][top : top + heads, left : left + rows] = scalars[p, owner].astype(
                    jnp.bfloat16
                )
            for j in range(2):
                column = pl.multiple_of((j * GROUPS + owner // span) * STATE, LANES)
                left = widths[0] + j * STATE
                outs[i][0:rows, left : left + STATE] = kq_near[:, pl.ds(column, STATE)]
    for copy in copies:
        copy.wait()


def mixer_kernel(peers, rows, heads, chunk, widths, whole_group, *refs):
    refs = list(refs)

    def take(count):
        taken = refs[:count]
        del refs[:count]
        return taken

    first = chunk == 0
    final = chunk == len(widths) - 1 and whole_group
    later = range(1, len(widths)) if first else ()
    width = widths[chunk]
    (me_ref,) = take(1)
    parts = take(peers)
    taps_ref, skip_ref = take(2)
    if not first:
        left_ref, b_ref, inward_ref, outward_ref, power_ref = take(5)
    if final:
        (gain_ref,) = take(1)
        earlier = take(chunk)
        (out_ref,) = take(1)
    else:
        total_ref, sums_ref = take(2)
    if first and later:
        left_ref, b_ref = take(2)
        inward_refs = take(len(later))
        outward_refs = take(len(later))
    wide, carry = take(2)
    if final:
        (total_ref,) = take(1)
    if first:
        (scalars,) = take(1)
    blocks = rows // BLOCK
    step = pl.program_id(0)
    me = me_ref[0]
    scale_rows = rows + 16 * blocks
    base = pl.multiple_of(step * rows, rows)
    scale_base = pl.multiple_of(step * scale_rows, 32)

    @pl.when(step == 0)
    def _():
        carry[...] = jnp.zeros_like(carry)
        wide[rows : rows + HALO] = jnp.zeros((HALO, wide.shape[1]), jnp.bfloat16)

    wide[0:HALO] = wide[rows : rows + HALO]
    ring = peers // 2
    slot = 2 * lax.rem(me // 2 + (ring - step // 2), ring) + ((me ^ step) & 1)
    for k in range(peers):

        @pl.when(slot == k)
        def _():
            if first:
                wide[HALO : HALO + rows] = parts[k][0:rows, 0 : wide.shape[1]]
                scalars[...] = parts[k][rows:, 0 : wide.shape[1]]
            else:
                wide[HALO : HALO + rows] = parts[k][0:rows, parts[k].shape[1] - width :]

    def spread(count):
        head_of = lax.broadcasted_iota(jnp.int32, (2 * count, count * HEAD_DIM), 1) // HEAD_DIM
        row = lax.rem(
            lax.broadcasted_iota(jnp.int32, (2 * count, count * HEAD_DIM), 0), count
        )
        return jnp.where(head_of == row, 1.0, 0.0).astype(jnp.bfloat16)

    def activated(top, size, lo, hi):
        rows_out = []
        for r in range(top, top + size, STRIP):
            lanes_out = []
            for lane in range(lo, hi, LANES):
                tap = [taps_ref[k : k + 1, lane : lane + LANES] for k in range(KW)]
                now = wide[r : r + STRIP + HALO, lane : lane + LANES].astype(jnp.float32)[HALO // 2 :]
                before = pltpu.roll(now, 1, 0)
                older = pltpu.roll(tap[0] * before + tap[1] * now, 2, 0)
                summed = (older + (tap[2] * before + tap[3] * now))[HALO // 2 :]
                lanes_out.append(
                    summed * pltpu.reciprocal(1.0 + jnp.exp(-summed), approx=True)
                )
            rows_out.append(jnp.concatenate(lanes_out, axis=1))
        return jnp.concatenate(rows_out, axis=0)

    if first:
        full = width + 2 * STATE
        across = full // rows
        row = lax.broadcasted_iota(jnp.int32, (rows, rows), 0)
        col = lax.broadcasted_iota(jnp.int32, (rows, rows), 1)
        lower = (row >= col) & (row // BLOCK == col // BLOCK)
        ones = jnp.where(lower, 1.0, 0.0).astype(jnp.bfloat16)
        eye = jnp.where(row == col, 1.0, 0.0).astype(jnp.bfloat16)

        def field(p):
            top = p // across * heads
            lane = p % across * rows
            return scalars[top : top + heads, lane : lane + rows]

        def by_rows(matrix, numbers):
            return sum(contract(matrix, field(p), ((1,), (1,))) for p in numbers)

        cumul = by_rows(ones, (0, 1))
        steps = by_rows(eye, (2,))
        middles = [
            cumul[b * BLOCK + BLOCK // 2 - 1 : b * BLOCK + BLOCK // 2] for b in range(blocks)
        ]
        middle = jnp.concatenate([jnp.broadcast_to(m, (BLOCK, heads)) for m in middles], axis=0)
        inward = as_parts(steps * jnp.exp(middle - cumul), 2)
        outward = as_parts(
            jnp.concatenate(
                [jnp.exp(cumul - middle)]
                + [jnp.broadcast_to(jnp.exp(m), (16, heads)) for m in middles],
                axis=0,
            ),
            2,
        )

        def chosen(halves, index):
            begin = sum(widths[:index]) // HEAD_DIM
            end = begin + widths[index] // HEAD_DIM
            return jnp.concatenate([half[:, begin:end] for half in halves], axis=1)

        bc = activated(0, rows, width, full).astype(jnp.bfloat16)
        b_part, c_part = bc[:, :STATE], bc[:, STATE:]
        scores = contract(c_part, b_part, ((1,), (1,)))
        scores = jnp.where(lower, scores, 0.0).astype(jnp.bfloat16)
        lefts = [
            jnp.concatenate(
                [
                    scores[b * BLOCK : (b + 1) * BLOCK, b * BLOCK : (b + 1) * BLOCK],
                    c_part[b * BLOCK : (b + 1) * BLOCK],
                ],
                axis=1,
            )
            for b in range(blocks)
        ]
        for index in later:
            inward_refs[index - 1][pl.ds(base, rows)] = chosen(inward, index)
            outward_refs[index - 1][pl.ds(scale_base, scale_rows)] = chosen(outward, index)
        if later:
            b_ref[pl.ds(base, rows)] = b_part
            for b in range(blocks):
                left_ref[pl.ds(base + b * BLOCK, BLOCK)] = lefts[b]
        inward = chosen(inward, 0)
        outward = chosen(outward, 0)
    else:
        inward = inward_ref[pl.ds(base, rows)]
        outward = outward_ref[pl.ds(scale_base, scale_rows)]
        b_part = b_ref[pl.ds(base, rows)]
        lefts = [left_ref[pl.ds(base + b * BLOCK, BLOCK)] for b in range(blocks)]

    tile = 2 * LANES if width % (2 * LANES) == 0 else LANES
    expand = spread(width // HEAD_DIM)
    compact = [
        jnp.concatenate(
            [
                inward[b * BLOCK : (b + 1) * BLOCK],
                outward[b * BLOCK : (b + 1) * BLOCK],
                outward[rows + 16 * b : rows + 16 * (b + 1)],
            ],
            axis=0,
        )
        for b in range(blocks)
    ]
    for b in range(blocks):
        top = b * BLOCK
        power = jnp.zeros((BLOCK, LANES), jnp.float32)
        if not first:
            power = power_ref[pl.ds(base + top, BLOCK)]
        for lo in range(0, width, tile):
            hi = lo + tile
            x_conv = activated(top, BLOCK, lo, hi)
            scales = contract(compact[b], expand[:, lo:hi], ((1,), (0,)))
            in_scale = scales[:BLOCK]
            out_scale = scales[BLOCK : 2 * BLOCK]
            mid_scale = scales[2 * BLOCK :]
            scaled = (x_conv * in_scale).astype(jnp.bfloat16)
            held = carry[:, lo:hi] * mid_scale[0:1]
            right = jnp.concatenate([scaled, held.astype(jnp.bfloat16)], axis=0)
            mixed = contract(lefts[b], right, ((1,), (0,)))
            total = mixed * out_scale + skip_ref[0:1, lo:hi] * x_conv
            if final:
                total_ref[top : top + BLOCK, lo:hi] = total
            else:
                total_ref[pl.ds(base + top, BLOCK), lo:hi] = total.astype(jnp.bfloat16)
            squares = total * total
            for lane in range(0, tile, LANES):
                power = power + squares[:, lane : lane + LANES]
            added = contract(b_part[top : top + BLOCK], scaled, ((0,), (0,)))
            carry[:, lo:hi] = (held + added) * out_scale[BLOCK - 1 : BLOCK]
        if final:
            summed = jnp.sum(power, axis=1, keepdims=True)
            norm = lax.rsqrt(summed * (1.0 / GROUP_WIDTH) + EPS)
            column = 0
            for index, size in enumerate(widths):
                if index < chunk:
                    block = earlier[index][pl.ds(base + top, BLOCK)].astype(jnp.float32)
                else:
                    block = total_ref[top : top + BLOCK]
                out_ref[top : top + BLOCK, column : column + size] = (
                    block * norm * gain_ref[0:1, column : column + size]
                ).astype(jnp.bfloat16)
                column += size
        else:
            sums_ref[pl.ds(base + top, BLOCK)] = power


def per_device(inputs, key_query, conv_inputs, conv_kq, step_size, decay_log, skip_gain, norm_gain):
    peers = lax.axis_size("ctx")
    me = lax.axis_index("ctx")
    place = me.reshape(1).astype(jnp.int32)
    rows = inputs.shape[0]
    owned = HEADS * HEAD_DIM // peers
    heads = HEADS // peers
    span = GROUP_WIDTH // owned
    whole_group = span == 1
    total_rows = peers * rows
    blocks = rows // BLOCK
    tiles = owned // LANES
    last = max(1, tiles // 2)
    widths = [(tiles - last) * LANES, last * LANES]
    offsets = [0, widths[0]]

    smem = pl.BlockSpec(memory_space=pltpu.SMEM)
    hbm = pl.BlockSpec(memory_space=pltpu.HBM)
    vmem = pl.BlockSpec(memory_space=pltpu.VMEM)
    params = pltpu.CompilerParams(vmem_limit_bytes=VMEM_LIMIT)

    def columns(a, first, size):
        return lax.dynamic_slice_in_dim(a, first, size, axis=1)

    lead = widths[0] + 2 * STATE
    scalar_rows = -(-(-(-FIELDS // (lead // rows)) * heads) // 16) * 16
    extents = {
        "full": (rows + scalar_rows, lead + widths[1]),
        "lead": (rows + scalar_rows, lead),
        "rest": (rows, widths[1]),
    }

    def pack(entries, after=()):
        token, _ = lax.optimization_barrier((place, after))
        heading = entries[0][1] != "rest"
        shapes = [jax.ShapeDtypeStruct(extents[kind], jnp.bfloat16) for _, kind in entries]
        operands = [token, inputs]
        in_specs = [smem, hbm]
        scratch = []
        if heading:
            operands += [key_query, decay_log, step_size]
            in_specs += [hbm] * 3
            scratch.append(pltpu.VMEM((2, rows, HEADS), jnp.float32))
            scratch.append(pltpu.VMEM((FIELDS, peers, heads, rows), jnp.float32))
            scratch.append(pltpu.VMEM(key_query.shape, jnp.bfloat16))
        scratch.append(pltpu.SemaphoreType.DMA((3, max(3, len(entries)))))
        return pl.pallas_call(
            functools.partial(
                pack_kernel,
                peers,
                span,
                widths,
                heads,
                entries,
                scalar_rows if heading else 0,
            ),
            in_specs=in_specs,
            out_specs=[vmem] * len(entries),
            out_shape=shapes,
            scratch_shapes=scratch,
            compiler_params=pltpu.CompilerParams(vmem_limit_bytes=PACK_VMEM),
            cost_estimate=pl.CostEstimate(
                flops=0,
                bytes_accessed=4 * sum(math.prod(shape.shape) for shape in shapes),
                transcendentals=0,
            ),
            name="pack",
        )(*operands)

    def send(message, code, after=()):
        message, _ = lax.optimization_barrier((message, after))
        pairs = [
            (i, 2 * ((i // 2 + code // 2) % (peers // 2)) + (i % 2 ^ code % 2))
            for i in range(peers)
        ]
        return lax.ppermute(message, "ctx", pairs)

    if peers == 8:
        one, two = pack(((4, "full"), (5, "full")))
        one, two = send(one, 2), send(two, 6)
        leads = pack(
            ((2, "lead"), (6, "lead"), (3, "lead"), (7, "lead"), (1, "full"), (0, "full"))
        )
        rests = pack(((2, "rest"), (6, "rest"), (3, "rest"), (7, "rest")), (one, two))
        lead = {0: leads[5], 1: send(leads[4], 1), 2: send(leads[0], 2), 6: send(leads[1], 6)}
        lead[4] = send(one, 2)
        lead[5] = send(two, 7)
        lead[3] = send(leads[2], 3, lead[2])
        lead[7] = send(leads[3], 7, lead[6])
        rest = {code: lead[code] for code in (0, 1, 4, 5)}
        rest[2] = send(rests[0], 2, lead[2])
        rest[6] = send(rests[1], 6, lead[6])
        rest[3] = send(rests[2], 3, lead[3])
        rest[7] = send(rests[3], 7, lead[7])
    else:
        codes = range(2, peers)
        packed = pack(((0, "full"), (1, "full")) + tuple((code, "lead") for code in codes))
        lead = {code: send(message, code) for code, message in enumerate(packed)}
        packed = pack(tuple((code, "rest") for code in codes), lead[peers - 1])
        rest = {0: lead[0], 1: lead[1]}
        rest.update((code, send(message, code)) for code, message in zip(codes, packed))
    received = [[slots[code] for code in range(peers)] for slots in (lead, rest)]

    taps_x = columns(conv_inputs, me * owned, owned)
    group = me // span
    taps_kq = jnp.concatenate(
        [
            columns(conv_kq, group * STATE, STATE),
            columns(conv_kq, (GROUPS + group) * STATE, STATE),
        ],
        axis=1,
    )
    skip = jnp.repeat(lax.dynamic_slice_in_dim(skip_gain, me * heads, heads), HEAD_DIM)[None]
    gain = columns(norm_gain[None], me * owned, owned)

    def by_source(count, lanes, dtype):
        spec = pl.BlockSpec((count, lanes), lambda i: (i, 0))
        return spec, jax.ShapeDtypeStruct((peers * count, lanes), dtype)

    def whole(count, lanes, dtype):
        return vmem, jax.ShapeDtypeStruct((peers * count, lanes), dtype)

    totals = []
    power = None
    shared = None
    for chunk, width in enumerate(widths):
        first = chunk == 0
        final = chunk == len(widths) - 1 and whole_group
        taps = taps_x[:, offsets[chunk] : offsets[chunk] + width]
        if first:
            taps = jnp.concatenate([taps, taps_kq], axis=1)
        cols = taps.shape[1]
        operands = [place, *received[chunk], taps, skip[:, offsets[chunk] : offsets[chunk] + width]]
        if not first:
            left, b_part, inward, outward = shared
            operands += [left, b_part, inward[chunk - 1], outward[chunk - 1], power]
        if final:
            operands += [gain, *totals]
        out = []
        if final:
            out.append(by_source(rows, owned, jnp.bfloat16))
        else:
            out.append(whole(rows, width, jnp.bfloat16))
            out.append(whole(rows, LANES, jnp.float32))
        if first:
            out.append(whole(rows, 2 * STATE, jnp.bfloat16))
            out.append(whole(rows, STATE, jnp.bfloat16))
            for count in (rows, rows + 16 * blocks):
                for size in widths[1:]:
                    out.append(whole(count, 2 * size // HEAD_DIM, jnp.bfloat16))
        scratch = [
            pltpu.VMEM((rows + HALO, cols), jnp.bfloat16),
            pltpu.VMEM((STATE, width), jnp.float32),
        ]
        if final:
            scratch.append(pltpu.VMEM((rows, width), jnp.float32))
        if first:
            scratch.append(pltpu.VMEM((scalar_rows, cols), jnp.bfloat16))
        results = pl.pallas_call(
            functools.partial(mixer_kernel, peers, rows, heads, chunk, widths, whole_group),
            grid=(peers,),
            in_specs=[smem] + [vmem] * (len(operands) - 1),
            out_specs=[spec for spec, _ in out],
            out_shape=[shape for _, shape in out],
            scratch_shapes=scratch,
            compiler_params=params,
            cost_estimate=pl.CostEstimate(
                flops=2 * total_rows * width * 450,
                bytes_accessed=total_rows * (2 * cols + 8 * width),
                transcendentals=total_rows * cols,
            ),
            name=f"mixer{chunk}",
        )(*operands)
        if final:
            return results[0]
        totals.append(results[0])
        power = results[1]
        if first:
            rest = results[4:]
            shared = (results[2], results[3], rest[: len(rest) // 2], rest[len(rest) // 2 :])
    sharers = [list(range(i, i + span)) for i in range(0, peers, span)]
    summed = jnp.sum(power, axis=1, keepdims=True)
    summed = lax.psum(summed, "ctx", axis_index_groups=sharers)
    total = jnp.concatenate(totals, axis=1)
    return (total * lax.rsqrt(summed * (1.0 / GROUP_WIDTH) + EPS) * gain).astype(jnp.bfloat16)


def solution(mesh):
    in_specs = (
        P(("dp", "ctx"), None),
        P(("dp", "ctx"), None),
        P(),
        P(),
        P(("dp", "ctx"), None),
        P(("dp", "ctx"), None),
        P(),
        P(),
    )
    out_specs = P("dp", "ctx")
    return jax.shard_map(
        per_device, mesh=mesh, in_specs=in_specs, out_specs=out_specs, check_vma=False
    )
```

profile of v0, /device:TPU:12, one launch (start us, length us, event | category | flops | bytes accessed | tf_op | source)
XLA Modules:
  0.0 133.6 jit_solution(1573022515176539585)
XLA Ops:
  0.0 0.0 copy-start.3
  0.0 2.8 %pack.4 = (bf16[272,1280]{1,0:T(8,128)(2,1)}, bf16[272,1280]{1,0:T(8,128)(2,1)}) custom-call(s32[1]{0:T(128)} %bitcast.refs_0_, bf16[256,8192]{1,0:T(8,128)(2,1)} %refs_1_.5, bf16[256,2048]{1,0:T(8,128)(2,1)} %refs_2_.3, f32[256,128]{1,0:T(8,128)} %refs_3_.3, f32[256,128]{1,0:T(8,128)} %refs_4_.3), custom_call_target="tpu_custom_call" | custom-call | bytes 2785280 | tf_op jit(solution)/shard_map/pack/pallas_call | solution.py:362
  2.8 0.5 collective-permute-start.2
  3.3 1.6 %collective-permute-start.1 = (bf16[272,1280]{1,0:T(8,128)(2,1)}, bf16[272,1280]{1,0:T(8,128)(2,1)}, u32[]{:S(2)}, u32[]{:S(2)}) collective-permute-start(bf16[272,1280]{1,0:T(8,128)(2,1)} %get-tuple-element.32), channel_id=1, source_target_pairs={{0,2},{1,3},{2,4},{3,5},{4,6},{5,7},{6,0},{7,1},{8,10},{9,11},{10,... | collective-permute-start | bytes 2088968 | tf_op jit(solution)/shard_map/ppermute | solution.py:391
  4.9 3.8 %pack.3 = (bf16[272,768]{1,0:T(8,128)(2,1)}, bf16[272,768]{1,0:T(8,128)(2,1)}, bf16[272,768]{1,0:T(8,128)(2,1)}, bf16[272,768]{1,0:T(8,128)(2,1)}, bf16[272,1280]{1,0:T(8,128)(2,1)}, /*index=5*/bf16[272,1280]{1,0:T(8,128)(2,1)}) custom-call(s32[1]{0:T(128)} %bitcast.refs_0_, bf16[256,8192]{1,0:T(8,128)(2,1)} %refs_1_.5, bf16[256,2048]{1,0:T(8,128)(2,1)} %refs_2_.3, ...), custom_call_target="tpu_custom_call" | custom-call | bytes 6127616 | tf_op jit(solution)/shard_map/pack/pallas_call | solution.py:362
  8.7 0.0 copy-start
  8.7 1.6 %collective-permute-start.3 = (bf16[272,768]{1,0:T(8,128)(2,1)}, bf16[272,768]{1,0:T(8,128)(2,1)S(1)}, u32[]{:S(2)}, u32[]{:S(2)}) collective-permute-start(bf16[272,768]{1,0:T(8,128)(2,1)} %get-tuple-element.36), channel_id=1, source_target_pairs={{0,2},{1,3},{2,4},{3,5},{4,6},{5,7},{6,0},{7,1},{8,10},{9,11},{10,... | collective-permute-start | bytes 1253384 | tf_op jit(solution)/shard_map/ppermute | solution.py:391
  10.3 0.5 collective-permute-start.9
  10.8 0.0 collective-permute-start
  10.8 33.7 %collective-permute-done.2 = bf16[272,1280]{1,0:T(8,128)(2,1)} collective-permute-done((bf16[272,1280]{1,0:T(8,128)(2,1)}, bf16[272,1280]{1,0:T(8,128)(2,1)}, u32[]{:S(2)}, u32[]{:S(2)}) %collective-permute-start.2) | collective-permute-done | bytes 696352 | tf_op jit(solution)/shard_map/ppermute | solution.py:391
  44.5 0.0 collective-permute-start.8
  44.5 0.0 collective-permute-done.1
  44.5 0.0 collective-permute-start.7
  44.5 3.0 %collective-permute-done.3.refs_3_ = bf16[272,768]{1,0:T(8,128)(2,1)S(1)} collective-permute-done((bf16[272,768]{1,0:T(8,128)(2,1)}, bf16[272,768]{1,0:T(8,128)(2,1)S(1)}, u32[]{:S(2)}, u32[]{:S(2)}) %collective-permute-start.3) | collective-permute-done | bytes 417824 | tf_op jit(solution)/shard_map/ppermute | solution.py:391
  47.5 0.0 collective-permute-start.5
  47.5 6.9 %collective-permute-done.9.refs_7_ = bf16[272,768]{1,0:T(8,128)(2,1)S(1)} collective-permute-done((bf16[272,768]{1,0:T(8,128)(2,1)}, bf16[272,768]{1,0:T(8,128)(2,1)S(1)}, u32[]{:S(2)}, u32[]{:S(2)}) %collective-permute-start.9) | collective-permute-done | bytes 417824 | tf_op jit(solution)/shard_map/ppermute | solution.py:391
  54.4 0.0 copy-start.1
  54.4 0.8 copy-done.1
  55.2 0.0 collective-permute-start.11
  55.2 0.7 dynamic-slice.3
  55.9 0.0 copy-done.3
  55.9 0.1 dynamic_slice.16
  56.0 0.1 broadcast_in_dim.4
  56.0 0.1 broadcast_in_dim_reshape.3
  56.1 0.0 copy-start.2
  56.1 0.8 constant_dynamic-slice_fusion.2
  56.9 0.7 constant_dynamic-slice_fusion.3
  57.6 2.3 %pack.5 = (bf16[256,512]{1,0:T(8,128)(2,1)}, bf16[256,512]{1,0:T(8,128)(2,1)}, bf16[256,512]{1,0:T(8,128)(2,1)}, bf16[256,512]{1,0:T(8,128)(2,1)}) custom-call(s32[1]{0:T(128)} %bitcast.refs_0_, bf16[256,8192]{1,0:T(8,128)(2,1)} %refs_1_.5), custom_call_target="tpu_custom_call" | custom-call | bytes 2097152 | tf_op jit(solution)/shard_map/pack/pallas_call | solution.py:362
  59.9 33.3 %collective-permute-done.5.refs_4_ = bf16[272,768]{1,0:T(8,128)(2,1)} collective-permute-done((bf16[272,768]{1,0:T(8,128)(2,1)}, bf16[272,768]{1,0:T(8,128)(2,1)}, u32[]{:S(2)}, u32[]{:S(2)}) %collective-permute-start.5) | collective-permute-done | bytes 417824 | tf_op jit(solution)/shard_map/ppermute | solution.py:391
  93.2 2.9 %collective-permute-start.4 = (bf16[256,512]{1,0:T(8,128)(2,1)}, bf16[256,512]{1,0:T(8,128)(2,1)S(1)}, u32[]{:S(2)}, u32[]{:S(2)}) collective-permute-start(bf16[256,512]{1,0:T(8,128)(2,1)} %get-tuple-element.37), channel_id=1, source_target_pairs={{0,2},{1,3},{2,4},{3,5},{4,6},{5,7},{6,0},{7,1},{8,10},{9,11},{10,... | collective-permute-start | bytes 786440 | tf_op jit(solution)/shard_map/ppermute | solution.py:391
  96.1 3.9 %collective-permute-done.11.refs_8_ = bf16[272,768]{1,0:T(8,128)(2,1)} collective-permute-done((bf16[272,768]{1,0:T(8,128)(2,1)}, bf16[272,768]{1,0:T(8,128)(2,1)}, u32[]{:S(2)}, u32[]{:S(2)}) %collective-permute-start.11) | collective-permute-done | bytes 417824 | tf_op jit(solution)/shard_map/ppermute | solution.py:391
  100.0 4.0 %collective-permute-start.10 = (bf16[256,512]{1,0:T(8,128)(2,1)}, bf16[256,512]{1,0:T(8,128)(2,1)S(1)}, u32[]{:S(2)}, u32[]{:S(2)}) collective-permute-start(bf16[256,512]{1,0:T(8,128)(2,1)} %get-tuple-element.44), channel_id=1, source_target_pairs={{0,6},{1,7},{2,0},{3,1},{4,2},{5,3},{6,4},{7,5},{8,14},{9,15},{10,... | collective-permute-start | bytes 786440 | tf_op jit(solution)/shard_map/ppermute | solution.py:391
  104.0 0.0 collective-permute-done.refs_2_
  104.0 0.0 collective-permute-start.6
  104.0 0.0 collective-permute-done.8.refs_6_
  104.0 3.5 %collective-permute-start.12 = (bf16[256,512]{1,0:T(8,128)(2,1)}, bf16[256,512]{1,0:T(8,128)(2,1)S(1)}, u32[]{:S(2)}, u32[]{:S(2)}) collective-permute-start(bf16[256,512]{1,0:T(8,128)(2,1)} %get-tuple-element.48), channel_id=1, source_target_pairs={{0,7},{1,6},{2,1},{3,0},{4,3},{5,2},{6,5},{7,4},{8,15},{9,14},{10,... | collective-permute-start | bytes 786440 | tf_op jit(solution)/shard_map/ppermute | solution.py:391
  107.5 0.0 collective-permute-done.7.refs_5_
  107.5 0.0 copy-done
  107.5 0.0 copy-done.2
  107.5 14.5 %mixer0.1 = (bf16[2048,512]{1,0:T(8,128)(2,1)S(1)}, f32[2048,128]{1,0:T(8,128)S(1)}, bf16[2048,256]{1,0:T(8,128)(2,1)S(1)}, bf16[2048,128]{1,0:T(8,128)(2,1)S(1)...) custom-call(s32[1]{0:T(128)} %bitcast.refs_0_, bf16[272,1280]{1,0:T(8,128)(2,1)S(1)} %copy-done, ...), custom_call_target="tpu_custom_call" | custom-call | flops 943718400 | bytes 11534336 | tf_op jit(solution)/shard_map/mixer0/pallas_call | solution.py:474
  121.9 0.0 collective-permute-done.4.refs_3_
  122.0 0.0 collective-permute-done.10.refs_7_
  122.0 0.0 collective-permute-done.6.refs_4_
  122.0 2.6 %collective-permute-done.12.refs_8_ = bf16[256,512]{1,0:T(8,128)(2,1)S(1)} collective-permute-done((bf16[256,512]{1,0:T(8,128)(2,1)}, bf16[256,512]{1,0:T(8,128)(2,1)S(1)}, u32[]{:S(2)}, u32[]{:S(2)}) %collective-permute-start.12) | collective-permute-done | bytes 262176 | tf_op jit(solution)/shard_map/ppermute | solution.py:391
  124.6 9.0 %mixer1.1 = bf16[2048,1024]{1,0:T(8,128)(2,1)} custom-call(s32[1]{0:T(128)} %bitcast.refs_0_, bf16[272,1280]{1,0:T(8,128)(2,1)S(1)} %copy-done, bf16[272,1280]{1,0:T(8,128)(2,1)S(1)} %collective-permute-done.refs_2_, bf16[256,512]{1,0:T(8,128)(2,1)S(1)} %collective-permute-done.4.refs_3_, bf16[256,512]{1,0:T(8,128)(2,1)S(1)} %collective-permute-done.6.refs_4_, ...), custom_call_target="tpu_custom_call" | custom-call | flops 943718400 | bytes 10485760 | tf_op jit(solution)/shard_map/mixer1/pallas_call | solution.py:474
  (2 shorter events, 0.0 us)
Async XLA Ops:
  0.0 55.9 %copy-start.3 = (f32[128]{0:T(128)S(1)}, f32[128]{0:T(128)}, u32[]{:S(2)}) copy-start(f32[128]{0:T(128)} %param.14) | copy-start | bytes 1540
  2.8 41.7 %collective-permute-start.2 = (bf16[272,1280]{1,0:T(8,128)(2,1)}, bf16[272,1280]{1,0:T(8,128)(2,1)}, u32[]{:S(2)}, u32[]{:S(2)}) collective-permute-start(bf16[272,1280]{1,0:T(8,128)(2,1)} %get-tuple-element.33), channel_id=1, source_target_pairs={{0,6},{1,7},{2,0},{3,1},{4,2},{5,3},{6,4},{7,5},{8,14},{9,15},{10,... | collective-permute-start | bytes 2088968 | tf_op jit(solution)/shard_map/ppermute | solution.py:391
  3.3 41.2 %collective-permute-start.1 = (bf16[272,1280]{1,0:T(8,128)(2,1)}, bf16[272,1280]{1,0:T(8,128)(2,1)}, u32[]{:S(2)}, u32[]{:S(2)}) collective-permute-start(bf16[272,1280]{1,0:T(8,128)(2,1)} %get-tuple-element.32), channel_id=1, source_target_pairs={{0,2},{1,3},{2,4},{3,5},{4,6},{5,7},{6,0},{7,1},{8,10},{9,11},{10,... | collective-permute-start | bytes 2088968 | tf_op jit(solution)/shard_map/ppermute | solution.py:391
  8.7 98.8 %copy-start = (bf16[272,1280]{1,0:T(8,128)(2,1)S(1)}, bf16[272,1280]{1,0:T(8,128)(2,1)}, u32[]{:S(2)}) copy-start(bf16[272,1280]{1,0:T(8,128)(2,1)} %get-tuple-element.30.refs_1_) | copy-start | bytes 2088964
  8.7 38.8 %collective-permute-start.3 = (bf16[272,768]{1,0:T(8,128)(2,1)}, bf16[272,768]{1,0:T(8,128)(2,1)S(1)}, u32[]{:S(2)}, u32[]{:S(2)}) collective-permute-start(bf16[272,768]{1,0:T(8,128)(2,1)} %get-tuple-element.36), channel_id=1, source_target_pairs={{0,2},{1,3},{2,4},{3,5},{4,6},{5,7},{6,0},{7,1},{8,10},{9,11},{10,... | collective-permute-start | bytes 1253384 | tf_op jit(solution)/shard_map/ppermute | solution.py:391
  10.3 44.1 %collective-permute-start.9 = (bf16[272,768]{1,0:T(8,128)(2,1)}, bf16[272,768]{1,0:T(8,128)(2,1)S(1)}, u32[]{:S(2)}, u32[]{:S(2)}) collective-permute-start(bf16[272,768]{1,0:T(8,128)(2,1)} %get-tuple-element.43), channel_id=1, source_target_pairs={{0,6},{1,7},{2,0},{3,1},{4,2},{5,3},{6,4},{7,5},{8,14},{9,15},{10,... | collective-permute-start | bytes 1253384 | tf_op jit(solution)/shard_map/ppermute | solution.py:391
  10.8 93.1 %collective-permute-start = (bf16[272,1280]{1,0:T(8,128)(2,1)}, bf16[272,1280]{1,0:T(8,128)(2,1)S(1)}, u32[]{:S(2)}, u32[]{:S(2)}) collective-permute-start(bf16[272,1280]{1,0:T(8,128)(2,1)} %get-tuple-element.31), channel_id=1, source_target_pairs={{0,1},{1,0},{2,3},{3,2},{4,5},{5,4},{6,7},{7,6},{8,9},{9,8},{10,11... | collective-permute-start | bytes 2088968 | tf_op jit(solution)/shard_map/ppermute | solution.py:391
  44.5 59.5 %collective-permute-start.8 = (bf16[272,1280]{1,0:T(8,128)(2,1)}, bf16[272,1280]{1,0:T(8,128)(2,1)S(1)}, u32[]{:S(2)}, u32[]{:S(2)}) collective-permute-start(bf16[272,1280]{1,0:T(8,128)(2,1)} %collective-permute-done.2), channel_id=1, source_target_pairs={{0,7},{1,6},{2,1},{3,0},{4,3},{5,2},{6,5},{7,4},{8,15},{9,14},{10,... | collective-permute-start | bytes 2088968 | tf_op jit(solution)/shard_map/ppermute | solution.py:391
  44.5 62.9 %collective-permute-start.7 = (bf16[272,1280]{1,0:T(8,128)(2,1)}, bf16[272,1280]{1,0:T(8,128)(2,1)S(1)}, u32[]{:S(2)}, u32[]{:S(2)}) collective-permute-start(bf16[272,1280]{1,0:T(8,128)(2,1)} %collective-permute-done.1), channel_id=1, source_target_pairs={{0,2},{1,3},{2,4},{3,5},{4,6},{5,7},{6,0},{7,1},{8,10},{9,11},{10,... | collective-permute-start | bytes 2088968 | tf_op jit(solution)/shard_map/ppermute | solution.py:391
  47.5 45.7 %collective-permute-start.5 = (bf16[272,768]{1,0:T(8,128)(2,1)}, bf16[272,768]{1,0:T(8,128)(2,1)}, u32[]{:S(2)}, u32[]{:S(2)}) collective-permute-start(bf16[272,768]{1,0:T(8,128)(2,1)} %get-tuple-element.40), channel_id=1, source_target_pairs={{0,3},{1,2},{2,5},{3,4},{4,7},{5,6},{6,1},{7,0},{8,11},{9,10},{10,... | collective-permute-start | bytes 1253384 | tf_op jit(solution)/shard_map/ppermute | solution.py:391
  54.4 0.8 copy-start.1
  55.2 44.8 %collective-permute-start.11 = (bf16[272,768]{1,0:T(8,128)(2,1)}, bf16[272,768]{1,0:T(8,128)(2,1)}, u32[]{:S(2)}, u32[]{:S(2)}) collective-permute-start(bf16[272,768]{1,0:T(8,128)(2,1)} %get-tuple-element.47), channel_id=1, source_target_pairs={{0,7},{1,6},{2,1},{3,0},{4,3},{5,2},{6,5},{7,4},{8,15},{9,14},{10,... | collective-permute-start | bytes 1253384 | tf_op jit(solution)/shard_map/ppermute | solution.py:391
  56.1 51.4 %copy-start.2 = (bf16[272,768]{1,0:T(8,128)(2,1)S(1)}, bf16[272,768]{1,0:T(8,128)(2,1)}, u32[]{:S(2)}) copy-start(bf16[272,768]{1,0:T(8,128)(2,1)} %copy-done.1) | copy-start | bytes 1253380
  93.2 28.7 %collective-permute-start.4 = (bf16[256,512]{1,0:T(8,128)(2,1)}, bf16[256,512]{1,0:T(8,128)(2,1)S(1)}, u32[]{:S(2)}, u32[]{:S(2)}) collective-permute-start(bf16[256,512]{1,0:T(8,128)(2,1)} %get-tuple-element.37), channel_id=1, source_target_pairs={{0,2},{1,3},{2,4},{3,5},{4,6},{5,7},{6,0},{7,1},{8,10},{9,11},{10,... | collective-permute-start | bytes 786440 | tf_op jit(solution)/shard_map/ppermute | solution.py:391
  100.0 22.0 %collective-permute-start.10 = (bf16[256,512]{1,0:T(8,128)(2,1)}, bf16[256,512]{1,0:T(8,128)(2,1)S(1)}, u32[]{:S(2)}, u32[]{:S(2)}) collective-permute-start(bf16[256,512]{1,0:T(8,128)(2,1)} %get-tuple-element.44), channel_id=1, source_target_pairs={{0,6},{1,7},{2,0},{3,1},{4,2},{5,3},{6,4},{7,5},{8,14},{9,15},{10,... | collective-permute-start | bytes 786440 | tf_op jit(solution)/shard_map/ppermute | solution.py:391
  104.0 18.0 %collective-permute-start.6 = (bf16[256,512]{1,0:T(8,128)(2,1)}, bf16[256,512]{1,0:T(8,128)(2,1)S(1)}, u32[]{:S(2)}, u32[]{:S(2)}) collective-permute-start(bf16[256,512]{1,0:T(8,128)(2,1)} %get-tuple-element.41), channel_id=1, source_target_pairs={{0,3},{1,2},{2,5},{3,4},{4,7},{5,6},{6,1},{7,0},{8,11},{9,10},{10,... | collective-permute-start | bytes 786440 | tf_op jit(solution)/shard_map/ppermute | solution.py:391
  104.0 20.6 %collective-permute-start.12 = (bf16[256,512]{1,0:T(8,128)(2,1)}, bf16[256,512]{1,0:T(8,128)(2,1)S(1)}, u32[]{:S(2)}, u32[]{:S(2)}) collective-permute-start(bf16[256,512]{1,0:T(8,128)(2,1)} %get-tuple-element.48), channel_id=1, source_target_pairs={{0,7},{1,6},{2,1},{3,0},{4,3},{5,2},{6,5},{7,4},{8,15},{9,14},{10,... | collective-permute-start | bytes 786440 | tf_op jit(solution)/shard_map/ppermute | solution.py:391
where the time goes:
time: 136 us; the launch traced here: 134 us
  waiting for transfers between devices  83.4 us (61%)
  Pallas kernels  32.3 us (24%)
  starting transfers between devices  14.6 us (11%)
  local copies, waits for them, and re-layouts  3.16 us (2%)
    ppermute x13, waiting for transfers between devices, send(): return lax.ppermute(message, 'ctx', pairs)  83.4 us
    pallas_call x2, Pallas kernels, per_device(): pl.pallas_call(functools.partial(mixer_kernel, peers, rows, heads, chunk,...  23.4 us
    ppermute x13, starting transfers between devices, send(): return lax.ppermute(message, 'ctx', pairs)  14.6 us
    pallas_call x3, Pallas kernels, pack(): pl.pallas_call(functools.partial(pack_kernel, peers, span, widths, heads,...  8.89 us
  transfers between devices with their start and end apart: 13, of which 6 were waited for; matrix products, arithmetic and copies ran while one was open for 2% of the time, Pallas kernels for 15%

commit v1 on v0

--- a/solution.py
+++ b/solution.py
@@ -38,7 +38,8 @@
 
 
 def relative(me, ring, code):
-    place = lax.rem(me // 2 + code // 2, ring)
+    hops = jnp.where((me & 1) == 0, code // 2, (ring - code // 2) % ring)
+    place = lax.rem(me // 2 + hops, ring)
     return 2 * place + ((me & 1) ^ (code & 1))
 
 
@@ -156,7 +157,9 @@
 
     wide[0:HALO] = wide[rows : rows + HALO]
     ring = peers // 2
-    slot = 2 * lax.rem(me // 2 + (ring - step // 2), ring) + ((me ^ step) & 1)
+    hops = lax.rem(me // 2 + (ring - step // 2), ring)
+    hops = jnp.where((step & 1) == 0, hops, lax.rem(ring - hops, ring))
+    slot = 2 * hops + ((me ^ step) & 1)
     for k in range(peers):
 
         @pl.when(slot == k)
@@ -384,8 +387,9 @@
 
     def send(message, code, after=()):
         message, _ = lax.optimization_barrier((message, after))
+        hops = (code // 2, -(code // 2))
         pairs = [
-            (i, 2 * ((i // 2 + code // 2) % (peers // 2)) + (i % 2 ^ code % 2))
+            (i, 2 * ((i // 2 + hops[i % 2]) % (peers // 2)) + (i % 2 ^ code % 2))
             for i in range(peers)
         ]
         return lax.ppermute(message, "ctx", pairs)

time: 136 us -> 138 us (1.015); the launches traced: 134 us -> 137 us
  waiting for transfers between devices: 83.4 us -> 86.3 us
    ppermute x13, waiting for transfers between devices: 83.4 us -> 86.3 us  [send(): return lax.ppermute(message, 'ctx', pairs)]
  transfers between devices with their start and end apart: 13 -> 13, of which waited for: 6 -> 7; matrix products, arithmetic and copies ran while one was open for 2% -> 2% of each run, Pallas kernels for 15% -> 15%
where the time goes in v1:
time: 138 us; the launch traced here: 137 us
  waiting for transfers between devices  86.3 us (63%)
  Pallas kernels  32.4 us (23%)
  starting transfers between devices  15.3 us (11%)
  local copies, waits for them, and re-layouts  3.16 us (2%)
    ppermute x13, waiting for transfers between devices, send(): return lax.ppermute(message, 'ctx', pairs)  86.3 us
    pallas_call x2, Pallas kernels, per_device(): pl.pallas_call(functools.partial(mixer_kernel, peers, rows, heads, chunk,...  23.5 us
    ppermute x13, starting transfers between devices, send(): return lax.ppermute(message, 'ctx', pairs)  15.3 us
    pallas_call x3, Pallas kernels, pack(): pl.pallas_call(functools.partial(pack_kernel, peers, span, widths, heads,...  8.89 us
  transfers between devices with their start and end apart: 13, of which 7 were waited for; matrix products, arithmetic and copies ran while one was open for 2% of the time, Pallas kernels for 15%

profile of v1, /device:TPU:12, one launch (start us, length us, event | category | flops | bytes accessed | tf_op | source)
XLA Modules:
  0.0 137.2 jit_solution(9609562481901082701)
XLA Ops:
  0.0 0.0 copy-start.3
  0.0 2.8 %pack.4 = (bf16[272,1280]{1,0:T(8,128)(2,1)}, bf16[272,1280]{1,0:T(8,128)(2,1)}) custom-call(s32[1]{0:T(128)} %bitcast.refs_0_, bf16[256,8192]{1,0:T(8,128)(2,1)} %refs_1_.5, bf16[256,2048]{1,0:T(8,128)(2,1)} %refs_2_.3, f32[256,128]{1,0:T(8,128)} %refs_3_.3, f32[256,128]{1,0:T(8,128)} %refs_4_.3), custom_call_target="tpu_custom_call" | custom-call | bytes 2785280 | tf_op jit(solution)/shard_map/pack/pallas_call | solution.py:365
  2.8 0.5 collective-permute-start.2
  3.3 1.6 %collective-permute-start.1 = (bf16[272,1280]{1,0:T(8,128)(2,1)}, bf16[272,1280]{1,0:T(8,128)(2,1)}, u32[]{:S(2)}, u32[]{:S(2)}) collective-permute-start(bf16[272,1280]{1,0:T(8,128)(2,1)} %get-tuple-element.32), channel_id=1, source_target_pairs={{0,2},{1,7},{2,4},{3,1},{4,6},{5,3},{6,0},{7,5},{8,10},{9,15},{10,... | collective-permute-start | bytes 2088968 | tf_op jit(solution)/shard_map/ppermute | solution.py:395
  4.9 3.8 %pack.3 = (bf16[272,768]{1,0:T(8,128)(2,1)}, bf16[272,768]{1,0:T(8,128)(2,1)}, bf16[272,768]{1,0:T(8,128)(2,1)}, bf16[272,768]{1,0:T(8,128)(2,1)}, bf16[272,1280]{1,0:T(8,128)(2,1)}, /*index=5*/bf16[272,1280]{1,0:T(8,128)(2,1)}) custom-call(s32[1]{0:T(128)} %bitcast.refs_0_, bf16[256,8192]{1,0:T(8,128)(2,1)} %refs_1_.5, bf16[256,2048]{1,0:T(8,128)(2,1)} %refs_2_.3, ...), custom_call_target="tpu_custom_call" | custom-call | bytes 6127616 | tf_op jit(solution)/shard_map/pack/pallas_call | solution.py:365
  8.7 0.0 copy-start
  8.7 1.6 %collective-permute-start.3 = (bf16[272,768]{1,0:T(8,128)(2,1)}, bf16[272,768]{1,0:T(8,128)(2,1)S(1)}, u32[]{:S(2)}, u32[]{:S(2)}) collective-permute-start(bf16[272,768]{1,0:T(8,128)(2,1)} %get-tuple-element.36), channel_id=1, source_target_pairs={{0,2},{1,7},{2,4},{3,1},{4,6},{5,3},{6,0},{7,5},{8,10},{9,15},{10,... | collective-permute-start | bytes 1253384 | tf_op jit(solution)/shard_map/ppermute | solution.py:395
  10.3 0.5 collective-permute-start.9
  10.8 0.0 collective-permute-start
  10.8 24.1 %collective-permute-done.2 = bf16[272,1280]{1,0:T(8,128)(2,1)} collective-permute-done((bf16[272,1280]{1,0:T(8,128)(2,1)}, bf16[272,1280]{1,0:T(8,128)(2,1)}, u32[]{:S(2)}, u32[]{:S(2)}) %collective-permute-start.2) | collective-permute-done | bytes 696352 | tf_op jit(solution)/shard_map/ppermute | solution.py:395
  35.0 0.0 collective-permute-start.8
  35.0 5.6 %collective-permute-done.1 = bf16[272,1280]{1,0:T(8,128)(2,1)} collective-permute-done((bf16[272,1280]{1,0:T(8,128)(2,1)}, bf16[272,1280]{1,0:T(8,128)(2,1)}, u32[]{:S(2)}, u32[]{:S(2)}) %collective-permute-start.1) | collective-permute-done | bytes 696352 | tf_op jit(solution)/shard_map/ppermute | solution.py:395
  40.6 2.6 %collective-permute-start.7 = (bf16[272,1280]{1,0:T(8,128)(2,1)}, bf16[272,1280]{1,0:T(8,128)(2,1)S(1)}, u32[]{:S(2)}, u32[]{:S(2)}) collective-permute-start(bf16[272,1280]{1,0:T(8,128)(2,1)} %collective-permute-done.1), channel_id=1, source_target_pairs={{0,2},{1,7},{2,4},{3,1},{4,6},{5,3},{6,0},{7,5},{8,10},{9,15},{10,... | collective-permute-start | bytes 2088968 | tf_op jit(solution)/shard_map/ppermute | solution.py:395
  43.2 8.9 %collective-permute-done.3.refs_3_ = bf16[272,768]{1,0:T(8,128)(2,1)S(1)} collective-permute-done((bf16[272,768]{1,0:T(8,128)(2,1)}, bf16[272,768]{1,0:T(8,128)(2,1)S(1)}, u32[]{:S(2)}, u32[]{:S(2)}) %collective-permute-start.3) | collective-permute-done | bytes 417824 | tf_op jit(solution)/shard_map/ppermute | solution.py:395
  52.1 2.2 %collective-permute-start.5 = (bf16[272,768]{1,0:T(8,128)(2,1)}, bf16[272,768]{1,0:T(8,128)(2,1)}, u32[]{:S(2)}, u32[]{:S(2)}) collective-permute-start(bf16[272,768]{1,0:T(8,128)(2,1)} %get-tuple-element.40), channel_id=1, source_target_pairs={{0,3},{1,6},{2,5},{3,0},{4,7},{5,2},{6,1},{7,4},{8,11},{9,14},{10,... | collective-permute-start | bytes 1253384 | tf_op jit(solution)/shard_map/ppermute | solution.py:395
  54.3 1.1 collective-permute-done.9.refs_7_
  55.4 0.0 copy-start.1
  55.4 0.8 copy-done.1
  56.2 1.9 %collective-permute-start.11 = (bf16[272,768]{1,0:T(8,128)(2,1)}, bf16[272,768]{1,0:T(8,128)(2,1)}, u32[]{:S(2)}, u32[]{:S(2)}) collective-permute-start(bf16[272,768]{1,0:T(8,128)(2,1)} %get-tuple-element.47), channel_id=1, source_target_pairs={{0,7},{1,2},{2,1},{3,4},{4,3},{5,6},{6,5},{7,0},{8,15},{9,10},{10,... | collective-permute-start | bytes 1253384 | tf_op jit(solution)/shard_map/ppermute | solution.py:395
  58.1 0.7 dynamic-slice.3
  58.7 0.0 copy-done.3
  58.8 0.1 dynamic_slice.16
  58.8 0.1 broadcast_in_dim.4
  58.9 0.1 broadcast_in_dim_reshape.3
  59.0 0.0 copy-start.2
  59.0 0.8 constant_dynamic-slice_fusion.2
  59.7 0.7 constant_dynamic-slice_fusion.3
  60.5 2.3 %pack.5 = (bf16[256,512]{1,0:T(8,128)(2,1)}, bf16[256,512]{1,0:T(8,128)(2,1)}, bf16[256,512]{1,0:T(8,128)(2,1)}, bf16[256,512]{1,0:T(8,128)(2,1)}) custom-call(s32[1]{0:T(128)} %bitcast.refs_0_, bf16[256,8192]{1,0:T(8,128)(2,1)} %refs_1_.5), custom_call_target="tpu_custom_call" | custom-call | bytes 2097152 | tf_op jit(solution)/shard_map/pack/pallas_call | solution.py:365
  62.8 39.2 %collective-permute-done.5.refs_4_ = bf16[272,768]{1,0:T(8,128)(2,1)} collective-permute-done((bf16[272,768]{1,0:T(8,128)(2,1)}, bf16[272,768]{1,0:T(8,128)(2,1)}, u32[]{:S(2)}, u32[]{:S(2)}) %collective-permute-start.5) | collective-permute-done | bytes 417824 | tf_op jit(solution)/shard_map/ppermute | solution.py:395
  102.0 0.0 collective-permute-start.4
  102.0 0.0 collective-permute-done.11.refs_8_
  102.0 2.0 %collective-permute-start.10 = (bf16[256,512]{1,0:T(8,128)(2,1)}, bf16[256,512]{1,0:T(8,128)(2,1)S(1)}, u32[]{:S(2)}, u32[]{:S(2)}) collective-permute-start(bf16[256,512]{1,0:T(8,128)(2,1)} %get-tuple-element.44), channel_id=1, source_target_pairs={{0,6},{1,3},{2,0},{3,5},{4,2},{5,7},{6,4},{7,1},{8,14},{9,11},{10,... | collective-permute-start | bytes 786440 | tf_op jit(solution)/shard_map/ppermute | solution.py:395
  104.0 0.0 collective-permute-done.refs_2_
  104.0 0.0 collective-permute-start.6
  104.0 0.0 collective-permute-done.8.refs_6_
  104.0 2.3 %collective-permute-start.12 = (bf16[256,512]{1,0:T(8,128)(2,1)}, bf16[256,512]{1,0:T(8,128)(2,1)S(1)}, u32[]{:S(2)}, u32[]{:S(2)}) collective-permute-start(bf16[256,512]{1,0:T(8,128)(2,1)} %get-tuple-element.48), channel_id=1, source_target_pairs={{0,7},{1,2},{2,1},{3,4},{4,3},{5,6},{6,5},{7,0},{8,15},{9,10},{10,... | collective-permute-start | bytes 786440 | tf_op jit(solution)/shard_map/ppermute | solution.py:395
  106.4 0.0 collective-permute-done.7.refs_5_
  106.4 0.0 copy-done
  106.4 0.0 copy-done.2
  106.4 14.5 %mixer0.1 = (bf16[2048,512]{1,0:T(8,128)(2,1)S(1)}, f32[2048,128]{1,0:T(8,128)S(1)}, bf16[2048,256]{1,0:T(8,128)(2,1)S(1)}, bf16[2048,128]{1,0:T(8,128)(2,1)S(1)...) custom-call(s32[1]{0:T(128)} %bitcast.refs_0_, bf16[272,1280]{1,0:T(8,128)(2,1)S(1)} %copy-done, ...), custom_call_target="tpu_custom_call" | custom-call | flops 943718400 | bytes 11534336 | tf_op jit(solution)/shard_map/mixer0/pallas_call | solution.py:478
  120.9 0.0 collective-permute-done.4.refs_3_
  120.9 0.0 collective-permute-done.10.refs_7_
  120.9 2.4 %collective-permute-done.6.refs_4_ = bf16[256,512]{1,0:T(8,128)(2,1)S(1)} collective-permute-done((bf16[256,512]{1,0:T(8,128)(2,1)}, bf16[256,512]{1,0:T(8,128)(2,1)S(1)}, u32[]{:S(2)}, u32[]{:S(2)}) %collective-permute-start.6) | collective-permute-done | bytes 262176 | tf_op jit(solution)/shard_map/ppermute | solution.py:395
  123.3 5.0 %collective-permute-done.12.refs_8_ = bf16[256,512]{1,0:T(8,128)(2,1)S(1)} collective-permute-done((bf16[256,512]{1,0:T(8,128)(2,1)}, bf16[256,512]{1,0:T(8,128)(2,1)S(1)}, u32[]{:S(2)}, u32[]{:S(2)}) %collective-permute-start.12) | collective-permute-done | bytes 262176 | tf_op jit(solution)/shard_map/ppermute | solution.py:395
  128.2 9.0 %mixer1.1 = bf16[2048,1024]{1,0:T(8,128)(2,1)} custom-call(s32[1]{0:T(128)} %bitcast.refs_0_, bf16[272,1280]{1,0:T(8,128)(2,1)S(1)} %copy-done, bf16[272,1280]{1,0:T(8,128)(2,1)S(1)} %collective-permute-done.refs_2_, bf16[256,512]{1,0:T(8,128)(2,1)S(1)} %collective-permute-done.4.refs_3_, bf16[256,512]{1,0:T(8,128)(2,1)S(1)} %collective-permute-done.6.refs_4_, ...), custom_call_target="tpu_custom_call" | custom-call | flops 943718400 | bytes 10485760 | tf_op jit(solution)/shard_map/mixer1/pallas_call | solution.py:478
  (2 shorter events, 0.0 us)
Async XLA Ops:
  0.0 58.7 %copy-start.3 = (f32[128]{0:T(128)S(1)}, f32[128]{0:T(128)}, u32[]{:S(2)}) copy-start(f32[128]{0:T(128)} %param.14) | copy-start | bytes 1540
  2.8 32.1 %collective-permute-start.2 = (bf16[272,1280]{1,0:T(8,128)(2,1)}, bf16[272,1280]{1,0:T(8,128)(2,1)}, u32[]{:S(2)}, u32[]{:S(2)}) collective-permute-start(bf16[272,1280]{1,0:T(8,128)(2,1)} %get-tuple-element.33), channel_id=1, source_target_pairs={{0,6},{1,3},{2,0},{3,5},{4,2},{5,7},{6,4},{7,1},{8,14},{9,11},{10,... | collective-permute-start | bytes 2088968 | tf_op jit(solution)/shard_map/ppermute | solution.py:395
  3.3 37.2 %collective-permute-start.1 = (bf16[272,1280]{1,0:T(8,128)(2,1)}, bf16[272,1280]{1,0:T(8,128)(2,1)}, u32[]{:S(2)}, u32[]{:S(2)}) collective-permute-start(bf16[272,1280]{1,0:T(8,128)(2,1)} %get-tuple-element.32), channel_id=1, source_target_pairs={{0,2},{1,7},{2,4},{3,1},{4,6},{5,3},{6,0},{7,5},{8,10},{9,15},{10,... | collective-permute-start | bytes 2088968 | tf_op jit(solution)/shard_map/ppermute | solution.py:395
  8.7 97.7 %copy-start = (bf16[272,1280]{1,0:T(8,128)(2,1)S(1)}, bf16[272,1280]{1,0:T(8,128)(2,1)}, u32[]{:S(2)}) copy-start(bf16[272,1280]{1,0:T(8,128)(2,1)} %get-tuple-element.30.refs_1_) | copy-start | bytes 2088964
  8.7 43.4 %collective-permute-start.3 = (bf16[272,768]{1,0:T(8,128)(2,1)}, bf16[272,768]{1,0:T(8,128)(2,1)S(1)}, u32[]{:S(2)}, u32[]{:S(2)}) collective-permute-start(bf16[272,768]{1,0:T(8,128)(2,1)} %get-tuple-element.36), channel_id=1, source_target_pairs={{0,2},{1,7},{2,4},{3,1},{4,6},{5,3},{6,0},{7,5},{8,10},{9,15},{10,... | collective-permute-start | bytes 1253384 | tf_op jit(solution)/shard_map/ppermute | solution.py:395
  10.3 45.1 %collective-permute-start.9 = (bf16[272,768]{1,0:T(8,128)(2,1)}, bf16[272,768]{1,0:T(8,128)(2,1)S(1)}, u32[]{:S(2)}, u32[]{:S(2)}) collective-permute-start(bf16[272,768]{1,0:T(8,128)(2,1)} %get-tuple-element.43), channel_id=1, source_target_pairs={{0,6},{1,3},{2,0},{3,5},{4,2},{5,7},{6,4},{7,1},{8,14},{9,11},{10,... | collective-permute-start | bytes 1253384 | tf_op jit(solution)/shard_map/ppermute | solution.py:395
  10.8 93.2 %collective-permute-start = (bf16[272,1280]{1,0:T(8,128)(2,1)}, bf16[272,1280]{1,0:T(8,128)(2,1)S(1)}, u32[]{:S(2)}, u32[]{:S(2)}) collective-permute-start(bf16[272,1280]{1,0:T(8,128)(2,1)} %get-tuple-element.31), channel_id=1, source_target_pairs={{0,1},{1,0},{2,3},{3,2},{4,5},{5,4},{6,7},{7,6},{8,9},{9,8},{10,11... | collective-permute-start | bytes 2088968 | tf_op jit(solution)/shard_map/ppermute | solution.py:395
  35.0 69.1 %collective-permute-start.8 = (bf16[272,1280]{1,0:T(8,128)(2,1)}, bf16[272,1280]{1,0:T(8,128)(2,1)S(1)}, u32[]{:S(2)}, u32[]{:S(2)}) collective-permute-start(bf16[272,1280]{1,0:T(8,128)(2,1)} %collective-permute-done.2), channel_id=1, source_target_pairs={{0,7},{1,2},{2,1},{3,4},{4,3},{5,6},{6,5},{7,0},{8,15},{9,10},{10,... | collective-permute-start | bytes 2088968 | tf_op jit(solution)/shard_map/ppermute | solution.py:395
  40.6 65.8 %collective-permute-start.7 = (bf16[272,1280]{1,0:T(8,128)(2,1)}, bf16[272,1280]{1,0:T(8,128)(2,1)S(1)}, u32[]{:S(2)}, u32[]{:S(2)}) collective-permute-start(bf16[272,1280]{1,0:T(8,128)(2,1)} %collective-permute-done.1), channel_id=1, source_target_pairs={{0,2},{1,7},{2,4},{3,1},{4,6},{5,3},{6,0},{7,5},{8,10},{9,15},{10,... | collective-permute-start | bytes 2088968 | tf_op jit(solution)/shard_map/ppermute | solution.py:395
  52.1 49.9 %collective-permute-start.5 = (bf16[272,768]{1,0:T(8,128)(2,1)}, bf16[272,768]{1,0:T(8,128)(2,1)}, u32[]{:S(2)}, u32[]{:S(2)}) collective-permute-start(bf16[272,768]{1,0:T(8,128)(2,1)} %get-tuple-element.40), channel_id=1, source_target_pairs={{0,3},{1,6},{2,5},{3,0},{4,7},{5,2},{6,1},{7,4},{8,11},{9,14},{10,... | collective-permute-start | bytes 1253384 | tf_op jit(solution)/shard_map/ppermute | solution.py:395
  55.4 0.8 copy-start.1
  56.2 45.8 %collective-permute-start.11 = (bf16[272,768]{1,0:T(8,128)(2,1)}, bf16[272,768]{1,0:T(8,128)(2,1)}, u32[]{:S(2)}, u32[]{:S(2)}) collective-permute-start(bf16[272,768]{1,0:T(8,128)(2,1)} %get-tuple-element.47), channel_id=1, source_target_pairs={{0,7},{1,2},{2,1},{3,4},{4,3},{5,6},{6,5},{7,0},{8,15},{9,10},{10,... | collective-permute-start | bytes 1253384 | tf_op jit(solution)/shard_map/ppermute | solution.py:395
  59.0 47.4 %copy-start.2 = (bf16[272,768]{1,0:T(8,128)(2,1)S(1)}, bf16[272,768]{1,0:T(8,128)(2,1)}, u32[]{:S(2)}) copy-start(bf16[272,768]{1,0:T(8,128)(2,1)} %copy-done.1) | copy-start | bytes 1253380
  102.0 18.9 %collective-permute-start.4 = (bf16[256,512]{1,0:T(8,128)(2,1)}, bf16[256,512]{1,0:T(8,128)(2,1)S(1)}, u32[]{:S(2)}, u32[]{:S(2)}) collective-permute-start(bf16[256,512]{1,0:T(8,128)(2,1)} %get-tuple-element.37), channel_id=1, source_target_pairs={{0,2},{1,7},{2,4},{3,1},{4,6},{5,3},{6,0},{7,5},{8,10},{9,15},{10,... | collective-permute-start | bytes 786440 | tf_op jit(solution)/shard_map/ppermute | solution.py:395
  102.0 18.9 %collective-permute-start.10 = (bf16[256,512]{1,0:T(8,128)(2,1)}, bf16[256,512]{1,0:T(8,128)(2,1)S(1)}, u32[]{:S(2)}, u32[]{:S(2)}) collective-permute-start(bf16[256,512]{1,0:T(8,128)(2,1)} %get-tuple-element.44), channel_id=1, source_target_pairs={{0,6},{1,3},{2,0},{3,5},{4,2},{5,7},{6,4},{7,1},{8,14},{9,11},{10,... | collective-permute-start | bytes 786440 | tf_op jit(solution)/shard_map/ppermute | solution.py:395
  104.0 19.3 %collective-permute-start.6 = (bf16[256,512]{1,0:T(8,128)(2,1)}, bf16[256,512]{1,0:T(8,128)(2,1)S(1)}, u32[]{:S(2)}, u32[]{:S(2)}) collective-permute-start(bf16[256,512]{1,0:T(8,128)(2,1)} %get-tuple-element.41), channel_id=1, source_target_pairs={{0,3},{1,6},{2,5},{3,0},{4,7},{5,2},{6,1},{7,4},{8,11},{9,14},{10,... | collective-permute-start | bytes 786440 | tf_op jit(solution)/shard_map/ppermute | solution.py:395
  104.0 24.2 %collective-permute-start.12 = (bf16[256,512]{1,0:T(8,128)(2,1)}, bf16[256,512]{1,0:T(8,128)(2,1)S(1)}, u32[]{:S(2)}, u32[]{:S(2)}) collective-permute-start(bf16[256,512]{1,0:T(8,128)(2,1)} %get-tuple-element.48), channel_id=1, source_target_pairs={{0,7},{1,2},{2,1},{3,4},{4,3},{5,6},{6,5},{7,0},{8,15},{9,10},{10,... | collective-permute-start | bytes 786440 | tf_op jit(solution)/shard_map/ppermute | solution.py:395

commit v2 on v0

--- a/solution.py
+++ b/solution.py
@@ -18,7 +18,8 @@
 EPS = 1e-05
 HALO = 16
 LANES = 128
-FIELDS = 3
+SUBLANES = 8
+FIELDS = 2
 STRIP = 64
 PACK_VMEM = 58 * 1024 * 1024
 VMEM_LIMIT = 32 * 1024 * 1024
@@ -37,9 +38,13 @@
     return parts
 
 
-def relative(me, ring, code):
-    place = lax.rem(me // 2 + code // 2, ring)
-    return 2 * place + ((me & 1) ^ (code & 1))
+def scalar_units(heads, rows, cols):
+    units = []
+    for p in range(FIELDS):
+        for head in range(0, heads, SUBLANES):
+            line, column = divmod(len(units), cols // rows)
+            units.append((p, head, min(SUBLANES, heads), line * SUBLANES, column * rows))
+    return units
 
 
 def pack_kernel(peers, span, widths, heads, entries, scalar_rows, *refs):
@@ -67,7 +72,7 @@
         loads.append(pltpu.make_async_copy(kq_ref, kq_near, sems.at[2, 2]))
         for load in loads:
             load.start()
-    owners = [relative(me, peers // 2, code) for code, _ in entries]
+    owners = [lax.rem(me + code, peers) for code, _ in entries]
     for i, (owner, (_, kind)) in enumerate(zip(owners, entries)):
         pieces = {
             "full": [(0, 0, 0), (1, widths[0], lead)],
@@ -88,20 +93,16 @@
     if heading:
         for load in loads:
             load.wait()
-        fields = as_parts(raw_scalars[0].T, 2) + as_parts(raw_scalars[1].T, 1)
+        fields = [raw_scalars[0].T, raw_scalars[1].T]
         for p, field in enumerate(fields):
-            field = field.astype(jnp.float32)
             for owner in range(peers):
                 scalars[p, owner] = field[owner * heads : (owner + 1) * heads]
-        across = lead // rows
         for i, owner in enumerate(owners):
             outs[i][rows:] = jnp.zeros((scalar_rows, outs[i].shape[1]), jnp.bfloat16)
-            for p in range(FIELDS):
-                top = rows + p // across * heads
-                left = p % across * rows
-                outs[i][top : top + heads, left : left + rows] = scalars[p, owner].astype(
-                    jnp.bfloat16
-                )
+            for p, head, count, top, left in scalar_units(heads, rows, lead):
+                outs[i][rows + top : rows + top + count, left : left + rows] = scalars[
+                    p, owner, head : head + count
+                ].astype(jnp.bfloat16)
             for j in range(2):
                 column = pl.multiple_of((j * GROUPS + owner // span) * STATE, LANES)
                 left = widths[0] + j * STATE
@@ -155,8 +156,7 @@
         wide[rows : rows + HALO] = jnp.zeros((HALO, wide.shape[1]), jnp.bfloat16)
 
     wide[0:HALO] = wide[rows : rows + HALO]
-    ring = peers // 2
-    slot = 2 * lax.rem(me // 2 + (ring - step // 2), ring) + ((me ^ step) & 1)
+    slot = lax.rem(me + (peers - step), peers)
     for k in range(peers):
 
         @pl.when(slot == k)
@@ -192,7 +192,6 @@
 
     if first:
         full = width + 2 * STATE
-        across = full // rows
         row = lax.broadcasted_iota(jnp.int32, (rows, rows), 0)
         col = lax.broadcasted_iota(jnp.int32, (rows, rows), 1)
         lower = (row >= col) & (row // BLOCK == col // BLOCK)
@@ -200,15 +199,15 @@
         eye = jnp.where(row == col, 1.0, 0.0).astype(jnp.bfloat16)
 
         def field(p):
-            top = p // across * heads
-            lane = p % across * rows
-            return scalars[top : top + heads, lane : lane + rows]
-
-        def by_rows(matrix, numbers):
-            return sum(contract(matrix, field(p), ((1,), (1,))) for p in numbers)
-
-        cumul = by_rows(ones, (0, 1))
-        steps = by_rows(eye, (2,))
+            pieces = [
+                scalars[top : top + count, left : left + rows].astype(jnp.float32)
+                for q, _, count, top, left in scalar_units(heads, rows, full)
+                if q == p
+            ]
+            return jnp.concatenate(pieces, axis=0).astype(jnp.bfloat16)
+
+        cumul = contract(ones, field(0), ((1,), (1,)))
+        steps = contract(eye, field(1), ((1,), (1,)))
         middles = [
             cumul[b * BLOCK + BLOCK // 2 - 1 : b * BLOCK + BLOCK // 2] for b in range(blocks)
         ]
@@ -325,7 +324,7 @@
     total_rows = peers * rows
     blocks = rows // BLOCK
     tiles = owned // LANES
-    last = max(1, tiles // 2)
+    last = max(1, tiles // 4)
     widths = [(tiles - last) * LANES, last * LANES]
     offsets = [0, widths[0]]
 
@@ -337,11 +336,11 @@
     def columns(a, first, size):
         return lax.dynamic_slice_in_dim(a, first, size, axis=1)
 
-    lead = widths[0] + 2 * STATE
-    scalar_rows = -(-(-(-FIELDS // (lead // rows)) * heads) // 16) * 16
+    lead_cols = widths[0] + 2 * STATE
+    scalar_rows = scalar_units(heads, rows, lead_cols)[-1][3] + SUBLANES
     extents = {
-        "full": (rows + scalar_rows, lead + widths[1]),
-        "lead": (rows + scalar_rows, lead),
+        "full": (rows + scalar_rows, lead_cols + widths[1]),
+        "lead": (rows + scalar_rows, lead_cols),
         "rest": (rows, widths[1]),
     }
 
@@ -384,36 +383,21 @@
 
     def send(message, code, after=()):
         message, _ = lax.optimization_barrier((message, after))
-        pairs = [
-            (i, 2 * ((i // 2 + code // 2) % (peers // 2)) + (i % 2 ^ code % 2))
-            for i in range(peers)
-        ]
+        pairs = [(i, (i + code) % peers) for i in range(peers)]
         return lax.ppermute(message, "ctx", pairs)
 
-    if peers == 8:
-        one, two = pack(((4, "full"), (5, "full")))
-        one, two = send(one, 2), send(two, 6)
-        leads = pack(
-            ((2, "lead"), (6, "lead"), (3, "lead"), (7, "lead"), (1, "full"), (0, "full"))
-        )
-        rests = pack(((2, "rest"), (6, "rest"), (3, "rest"), (7, "rest")), (one, two))
-        lead = {0: leads[5], 1: send(leads[4], 1), 2: send(leads[0], 2), 6: send(leads[1], 6)}
-        lead[4] = send(one, 2)
-        lead[5] = send(two, 7)
-        lead[3] = send(leads[2], 3, lead[2])
-        lead[7] = send(leads[3], 7, lead[6])
-        rest = {code: lead[code] for code in (0, 1, 4, 5)}
-        rest[2] = send(rests[0], 2, lead[2])
-        rest[6] = send(rests[1], 6, lead[6])
-        rest[3] = send(rests[2], 3, lead[3])
-        rest[7] = send(rests[3], 7, lead[7])
-    else:
-        codes = range(2, peers)
-        packed = pack(((0, "full"), (1, "full")) + tuple((code, "lead") for code in codes))
-        lead = {code: send(message, code) for code, message in enumerate(packed)}
-        packed = pack(tuple((code, "rest") for code in codes), lead[peers - 1])
-        rest = {0: lead[0], 1: lead[1]}
-        rest.update((code, send(message, code)) for code, message in zip(codes, packed))
+    far = sorted(range(2, peers - 1), key=lambda code: abs(code - peers // 2))
+    near = [1, peers - 1]
+    lead = {}
+    for code, message in zip(far, pack([(code, "lead") for code in far])):
+        lead[code] = send(message, code)
+    *packed, lead[0] = pack([(code, "full") for code in near] + [(0, "full")], lead[far[0]])
+    for code, message in zip(near, packed):
+        lead[code] = send(message, code)
+    rest = {code: lead[code] for code in near + [0]}
+    packed = pack([(code, "rest") for code in far], lead[far[0]])
+    for code, message in zip(far, packed):
+        rest[code] = send(message, code, lead[code])
     received = [[slots[code] for code in range(peers)] for slots in (lead, rest)]
 
     taps_x = columns(conv_inputs, me * owned, owned)

time: 136 us -> 139 us (1.022)
  starting transfers between devices: 14.6 us -> 26.9 us
  waiting for transfers between devices: 83.4 us -> 75.8 us
  local copies, waits for them, and re-layouts: 3.16 us -> 1.64 us
    ppermute x13 -> x12, starting transfers between devices: 14.6 us -> 26.9 us  [send(): return lax.ppermute(message, 'ctx', pairs)]
    ppermute x13 -> x12, waiting for transfers between devices: 83.4 us -> 75.8 us  [send(): return lax.ppermute(message, 'ctx', pairs)]
  transfers between devices with their start and end apart: 13 -> 12, of which waited for: 6 -> 3; matrix products, arithmetic and copies ran while one was open for 2% -> 1% of each run, Pallas kernels for 15% -> 16%
where the time goes in v2:
time: 139 us; the launch traced here: 138 us
  waiting for transfers between devices  75.8 us (55%)
  Pallas kernels  33.1 us (24%)
  starting transfers between devices  26.9 us (19%)
  local copies, waits for them, and re-layouts  1.64 us (1%)
    ppermute x12, waiting for transfers between devices, send(): return lax.ppermute(message, 'ctx', pairs)  75.8 us
    ppermute x12, starting transfers between devices, send(): return lax.ppermute(message, 'ctx', pairs)  26.9 us
    pallas_call x2, Pallas kernels, per_device(): pl.pallas_call(functools.partial(mixer_kernel, peers, rows, heads, chunk,...  24.2 us
    pallas_call x3, Pallas kernels, pack(): pl.pallas_call(functools.partial(pack_kernel, peers, span, widths, heads,...  8.94 us
  transfers between devices with their start and end apart: 12, of which 3 were waited for; matrix products, arithmetic and copies ran while one was open for 1% of the time, Pallas kernels for 16%

profile of v2, /device:TPU:12, one launch (start us, length us, event | category | flops | bytes accessed | tf_op | source)
XLA Modules:
  0.0 137.6 jit_solution(1427869035926046023)
XLA Ops:
  0.0 0.0 copy-start
  0.0 0.0 copy-start.2
  0.0 3.6 %pack.3 = (bf16[264,1024]{1,0:T(8,128)(2,1)}, bf16[264,1024]{1,0:T(8,128)(2,1)}, bf16[264,1024]{1,0:T(8,128)(2,1)}, bf16[264,1024]{1,0:T(8,128)(2,1)}, bf16[264,1024]{1,0:T(8,128)(2,1)}) custom-call(s32[1]{0:T(128)} %bitcast.refs_0_, bf16[256,8192]{1,0:T(8,128)(2,1)} %refs_1_.5, bf16[256,2048]{1,0:T(8,128)(2,1)} %refs_2_.3, f32[256,128]{1,0:T(8,128)} %refs_3_.3, ...), custom_call_target="tpu_custom_call" | custom-call | bytes 5406720 | tf_op jit(solution)/shard_map/pack/pallas_call | solution.py:361
  3.6 2.7 %collective-permute-start = (bf16[264,1024]{1,0:T(8,128)(2,1)}, bf16[264,1024]{1,0:T(8,128)(2,1)S(1)}, u32[]{:S(2)}, u32[]{:S(2)}) collective-permute-start(bf16[264,1024]{1,0:T(8,128)(2,1)} %get-tuple-element.30), channel_id=1, source_target_pairs={{0,4},{1,5},{2,6},{3,7},{4,0},{5,1},{6,2},{7,3},{8,12},{9,13},{10,... | collective-permute-start | bytes 1622024 | tf_op jit(solution)/shard_map/ppermute | solution.py:387
  6.3 0.0 collective-permute-start.2
  6.3 23.4 %collective-permute-done.refs_5_ = bf16[264,1024]{1,0:T(8,128)(2,1)S(1)} collective-permute-done((bf16[264,1024]{1,0:T(8,128)(2,1)}, bf16[264,1024]{1,0:T(8,128)(2,1)S(1)}, u32[]{:S(2)}, u32[]{:S(2)}) %collective-permute-start) | collective-permute-done | bytes 540704 | tf_op jit(solution)/shard_map/ppermute | solution.py:387
  29.7 3.2 %pack.4 = (bf16[264,1280]{1,0:T(8,128)(2,1)}, bf16[264,1280]{1,0:T(8,128)(2,1)}, bf16[264,1280]{1,0:T(8,128)(2,1)}) custom-call(s32[1]{0:T(128)} %bitcast.refs_0_, bf16[256,8192]{1,0:T(8,128)(2,1)} %refs_1_.5, bf16[256,2048]{1,0:T(8,128)(2,1)} %refs_2_.3, f32[256,128]{1,0:T(8,128)} %refs_3_.3, f32[256,128]{1,0:T(8,128)} %refs_4_.3), custom_call_target="tpu_custom_call" | custom-call | bytes 4055040 | tf_op jit(solution)/shard_map/pack/pallas_call | solution.py:361
  32.9 0.0 copy-start.1
  32.9 11.4 %collective-permute-start.11 = (bf16[264,1280]{1,0:T(8,128)(2,1)}, bf16[264,1280]{1,0:T(8,128)(2,1)S(1)}, u32[]{:S(2)}, u32[]{:S(2)}) collective-permute-start(bf16[264,1280]{1,0:T(8,128)(2,1)} %get-tuple-element.48), channel_id=1, source_target_pairs={{0,7},{1,0},{2,1},{3,2},{4,3},{5,4},{6,5},{7,6},{8,15},{9,8},{10,9... | collective-permute-start | bytes 2027528 | tf_op jit(solution)/shard_map/ppermute | solution.py:387
  44.3 0.0 collective-permute-start.1
  44.3 0.0 collective-permute-start.4
  44.3 3.6 %collective-permute-start.7 = (bf16[264,1024]{1,0:T(8,128)(2,1)}, bf16[264,1024]{1,0:T(8,128)(2,1)}, u32[]{:S(2)}, u32[]{:S(2)}) collective-permute-start(bf16[264,1024]{1,0:T(8,128)(2,1)} %get-tuple-element.43), channel_id=1, source_target_pairs={{0,5},{1,6},{2,7},{3,0},{4,1},{5,2},{6,3},{7,4},{8,13},{9,14},{10,... | collective-permute-start | bytes 1622024 | tf_op jit(solution)/shard_map/ppermute | solution.py:387
  47.8 0.0 collective-permute-done.2.refs_3_
  47.8 1.0 collective-permute-start.9
  48.8 0.0 copy-done.2
  48.8 0.1 dynamic_slice.16
  48.9 0.1 broadcast_in_dim.4
  49.0 0.1 broadcast_in_dim_reshape.3
  49.1 0.7 dynamic-slice.3
  49.8 0.0 copy-done
  49.8 0.7 constant_dynamic-slice_fusion.2
  50.5 2.2 %pack.5 = (bf16[256,256]{1,0:T(8,128)(2,1)}, bf16[256,256]{1,0:T(8,128)(2,1)}, bf16[256,256]{1,0:T(8,128)(2,1)}, bf16[256,256]{1,0:T(8,128)(2,1)}, bf16[256,256]{1,0:T(8,128)(2,1)}) custom-call(s32[1]{0:T(128)} %bitcast.refs_0_, bf16[256,8192]{1,0:T(8,128)(2,1)} %refs_1_.5), custom_call_target="tpu_custom_call" | custom-call | bytes 1310720 | tf_op jit(solution)/shard_map/pack/pallas_call | solution.py:361
  52.6 23.0 %collective-permute-done.4.refs_4_ = bf16[264,1024]{1,0:T(8,128)(2,1)} collective-permute-done((bf16[264,1024]{1,0:T(8,128)(2,1)}, bf16[264,1024]{1,0:T(8,128)(2,1)}, u32[]{:S(2)}, u32[]{:S(2)}) %collective-permute-start.4) | collective-permute-done | bytes 540704 | tf_op jit(solution)/shard_map/ppermute | solution.py:387
  75.6 29.4 %collective-permute-done.7.refs_6_ = bf16[264,1024]{1,0:T(8,128)(2,1)} collective-permute-done((bf16[264,1024]{1,0:T(8,128)(2,1)}, bf16[264,1024]{1,0:T(8,128)(2,1)}, u32[]{:S(2)}, u32[]{:S(2)}) %collective-permute-start.7) | collective-permute-done | bytes 540704 | tf_op jit(solution)/shard_map/ppermute | solution.py:387
  105.0 0.0 collective-permute-done.9.refs_7_
  105.0 0.0 collective-permute-start.10
  105.0 3.1 %collective-permute-start.8 = (bf16[256,256]{1,0:T(8,128)(2,1)}, bf16[256,256]{1,0:T(8,128)(2,1)S(1)}, u32[]{:S(2)}, u32[]{:S(2)}) collective-permute-start(bf16[256,256]{1,0:T(8,128)(2,1)} %get-tuple-element.44), channel_id=1, source_target_pairs={{0,5},{1,6},{2,7},{3,0},{4,1},{5,2},{6,3},{7,4},{8,13},{9,14},{10,... | collective-permute-start | bytes 393224 | tf_op jit(solution)/shard_map/ppermute | solution.py:387
  108.1 1.0 collective-permute-start.6
  109.1 0.0 collective-permute-done.11.refs_8_
  109.1 2.3 %collective-permute-start.5 = (bf16[256,256]{1,0:T(8,128)(2,1)}, bf16[256,256]{1,0:T(8,128)(2,1)S(1)}, u32[]{:S(2)}, u32[]{:S(2)}) collective-permute-start(bf16[256,256]{1,0:T(8,128)(2,1)} %get-tuple-element.39), channel_id=1, source_target_pairs={{0,3},{1,4},{2,5},{3,6},{4,7},{5,0},{6,1},{7,2},{8,11},{9,12},{10,... | collective-permute-start | bytes 393224 | tf_op jit(solution)/shard_map/ppermute | solution.py:387
  111.4 0.0 collective-permute-done.1.refs_2_
  111.4 2.0 %collective-permute-start.3 = (bf16[256,256]{1,0:T(8,128)(2,1)}, bf16[256,256]{1,0:T(8,128)(2,1)S(1)}, u32[]{:S(2)}, u32[]{:S(2)}) collective-permute-start(bf16[256,256]{1,0:T(8,128)(2,1)} %get-tuple-element.36), channel_id=1, source_target_pairs={{0,2},{1,3},{2,4},{3,5},{4,6},{5,7},{6,0},{7,1},{8,10},{9,11},{10,... | collective-permute-start | bytes 393224 | tf_op jit(solution)/shard_map/ppermute | solution.py:387
  113.4 0.0 copy-done.1
  113.4 16.9 %mixer0.1 = (bf16[2048,768]{1,0:T(8,128)(2,1)S(1)}, f32[2048,128]{1,0:T(8,128)S(1)}, bf16[2048,256]{1,0:T(8,128)(2,1)S(1)}, bf16[2048,128]{1,0:T(8,128)(2,1)S(1)...) custom-call(s32[1]{0:T(128)} %bitcast.refs_0_, bf16[264,1280]{1,0:T(8,128)(2,1)S(1)} %copy-done.1, ...), custom_call_target="tpu_custom_call" | custom-call | flops 1415577600 | bytes 16777216 | tf_op jit(solution)/shard_map/mixer0/pallas_call | solution.py:458
  130.3 0.0 collective-permute-done.10.refs_7_
  130.3 0.0 collective-permute-done.8.refs_6_
  130.3 0.0 collective-permute-done.6.refs_5_
  130.3 0.0 collective-permute-done.5.refs_4_
  130.3 0.0 collective-permute-done.3.refs_3_
  130.3 7.3 %mixer1.1 = bf16[2048,1024]{1,0:T(8,128)(2,1)} custom-call(s32[1]{0:T(128)} %bitcast.refs_0_, bf16[264,1280]{1,0:T(8,128)(2,1)S(1)} %copy-done.1, bf16[264,1280]{1,0:T(8,128)(2,1)S(1)} %collective-permute-done.1.refs_2_, bf16[256,256]{1,0:T(8,128)(2,1)S(1)} %collective-permute-done.3.refs_3_, bf16[256,256]{1,0:T(8,128)(2,1)S(1)} %collective-permute-done.5.refs_4_, ...), custom_call_target="tpu_custom_call" | custom-call | flops 471859200 | bytes 5242880 | tf_op jit(solution)/shard_map/mixer1/pallas_call | solution.py:458
  (5 shorter events, 0.0 us)
Async XLA Ops:
  0.0 49.8 %copy-start = (f32[4,8192]{1,0:T(4,128)S(1)}, f32[4,8192]{1,0:T(4,128)}, u32[]{:S(2)}) copy-start(f32[4,8192]{1,0:T(4,128)} %param.10) | copy-start | bytes 393220
  0.0 48.8 %copy-start.2 = (f32[128]{0:T(128)S(1)}, f32[128]{0:T(128)}, u32[]{:S(2)}) copy-start(f32[128]{0:T(128)} %param.14) | copy-start | bytes 1540
  3.6 26.1 %collective-permute-start = (bf16[264,1024]{1,0:T(8,128)(2,1)}, bf16[264,1024]{1,0:T(8,128)(2,1)S(1)}, u32[]{:S(2)}, u32[]{:S(2)}) collective-permute-start(bf16[264,1024]{1,0:T(8,128)(2,1)} %get-tuple-element.30), channel_id=1, source_target_pairs={{0,4},{1,5},{2,6},{3,7},{4,0},{5,1},{6,2},{7,3},{8,12},{9,13},{10,... | collective-permute-start | bytes 1622024 | tf_op jit(solution)/shard_map/ppermute | solution.py:387
  6.3 41.5 %collective-permute-start.2 = (bf16[264,1024]{1,0:T(8,128)(2,1)}, bf16[264,1024]{1,0:T(8,128)(2,1)S(1)}, u32[]{:S(2)}, u32[]{:S(2)}) collective-permute-start(bf16[264,1024]{1,0:T(8,128)(2,1)} %get-tuple-element.35), channel_id=1, source_target_pairs={{0,2},{1,3},{2,4},{3,5},{4,6},{5,7},{6,0},{7,1},{8,10},{9,11},{10,... | collective-permute-start | bytes 1622024 | tf_op jit(solution)/shard_map/ppermute | solution.py:387
  32.9 80.5 %copy-start.1 = (bf16[264,1280]{1,0:T(8,128)(2,1)S(1)}, bf16[264,1280]{1,0:T(8,128)(2,1)}, u32[]{:S(2)}) copy-start(bf16[264,1280]{1,0:T(8,128)(2,1)} %get-tuple-element.32.refs_1_) | copy-start | bytes 2027524
  32.9 76.2 %collective-permute-start.11 = (bf16[264,1280]{1,0:T(8,128)(2,1)}, bf16[264,1280]{1,0:T(8,128)(2,1)S(1)}, u32[]{:S(2)}, u32[]{:S(2)}) collective-permute-start(bf16[264,1280]{1,0:T(8,128)(2,1)} %get-tuple-element.48), channel_id=1, source_target_pairs={{0,7},{1,0},{2,1},{3,2},{4,3},{5,4},{6,5},{7,6},{8,15},{9,8},{10,9... | collective-permute-start | bytes 2027528 | tf_op jit(solution)/shard_map/ppermute | solution.py:387
  44.3 67.1 %collective-permute-start.1 = (bf16[264,1280]{1,0:T(8,128)(2,1)}, bf16[264,1280]{1,0:T(8,128)(2,1)S(1)}, u32[]{:S(2)}, u32[]{:S(2)}) collective-permute-start(bf16[264,1280]{1,0:T(8,128)(2,1)} %get-tuple-element.33), channel_id=1, source_target_pairs={{0,1},{1,2},{2,3},{3,4},{4,5},{5,6},{6,7},{7,0},{8,9},{9,10},{10,1... | collective-permute-start | bytes 2027528 | tf_op jit(solution)/shard_map/ppermute | solution.py:387
  44.3 31.3 %collective-permute-start.4 = (bf16[264,1024]{1,0:T(8,128)(2,1)}, bf16[264,1024]{1,0:T(8,128)(2,1)}, u32[]{:S(2)}, u32[]{:S(2)}) collective-permute-start(bf16[264,1024]{1,0:T(8,128)(2,1)} %get-tuple-element.38), channel_id=1, source_target_pairs={{0,3},{1,4},{2,5},{3,6},{4,7},{5,0},{6,1},{7,2},{8,11},{9,12},{10,... | collective-permute-start | bytes 1622024 | tf_op jit(solution)/shard_map/ppermute | solution.py:387
  44.3 60.8 %collective-permute-start.7 = (bf16[264,1024]{1,0:T(8,128)(2,1)}, bf16[264,1024]{1,0:T(8,128)(2,1)}, u32[]{:S(2)}, u32[]{:S(2)}) collective-permute-start(bf16[264,1024]{1,0:T(8,128)(2,1)} %get-tuple-element.43), channel_id=1, source_target_pairs={{0,5},{1,6},{2,7},{3,0},{4,1},{5,2},{6,3},{7,4},{8,13},{9,14},{10,... | collective-permute-start | bytes 1622024 | tf_op jit(solution)/shard_map/ppermute | solution.py:387
  47.8 57.2 %collective-permute-start.9 = (bf16[264,1024]{1,0:T(8,128)(2,1)}, bf16[264,1024]{1,0:T(8,128)(2,1)}, u32[]{:S(2)}, u32[]{:S(2)}) collective-permute-start(bf16[264,1024]{1,0:T(8,128)(2,1)} %get-tuple-element.46), channel_id=1, source_target_pairs={{0,6},{1,7},{2,0},{3,1},{4,2},{5,3},{6,4},{7,5},{8,14},{9,15},{10,... | collective-permute-start | bytes 1622024 | tf_op jit(solution)/shard_map/ppermute | solution.py:387
  105.0 25.3 %collective-permute-start.10 = (bf16[256,256]{1,0:T(8,128)(2,1)}, bf16[256,256]{1,0:T(8,128)(2,1)S(1)}, u32[]{:S(2)}, u32[]{:S(2)}) collective-permute-start(bf16[256,256]{1,0:T(8,128)(2,1)} %get-tuple-element.47), channel_id=1, source_target_pairs={{0,6},{1,7},{2,0},{3,1},{4,2},{5,3},{6,4},{7,5},{8,14},{9,15},{10,... | collective-permute-start | bytes 393224 | tf_op jit(solution)/shard_map/ppermute | solution.py:387
  105.0 25.3 %collective-permute-start.8 = (bf16[256,256]{1,0:T(8,128)(2,1)}, bf16[256,256]{1,0:T(8,128)(2,1)S(1)}, u32[]{:S(2)}, u32[]{:S(2)}) collective-permute-start(bf16[256,256]{1,0:T(8,128)(2,1)} %get-tuple-element.44), channel_id=1, source_target_pairs={{0,5},{1,6},{2,7},{3,0},{4,1},{5,2},{6,3},{7,4},{8,13},{9,14},{10,... | collective-permute-start | bytes 393224 | tf_op jit(solution)/shard_map/ppermute | solution.py:387
  108.1 22.2 %collective-permute-start.6 = (bf16[256,256]{1,0:T(8,128)(2,1)}, bf16[256,256]{1,0:T(8,128)(2,1)S(1)}, u32[]{:S(2)}, u32[]{:S(2)}) collective-permute-start(bf16[256,256]{1,0:T(8,128)(2,1)} %get-tuple-element.41), channel_id=1, source_target_pairs={{0,4},{1,5},{2,6},{3,7},{4,0},{5,1},{6,2},{7,3},{8,12},{9,13},{10,... | collective-permute-start | bytes 393224 | tf_op jit(solution)/shard_map/ppermute | solution.py:387
  109.1 21.2 %collective-permute-start.5 = (bf16[256,256]{1,0:T(8,128)(2,1)}, bf16[256,256]{1,0:T(8,128)(2,1)S(1)}, u32[]{:S(2)}, u32[]{:S(2)}) collective-permute-start(bf16[256,256]{1,0:T(8,128)(2,1)} %get-tuple-element.39), channel_id=1, source_target_pairs={{0,3},{1,4},{2,5},{3,6},{4,7},{5,0},{6,1},{7,2},{8,11},{9,12},{10,... | collective-permute-start | bytes 393224 | tf_op jit(solution)/shard_map/ppermute | solution.py:387
  111.4 18.9 %collective-permute-start.3 = (bf16[256,256]{1,0:T(8,128)(2,1)}, bf16[256,256]{1,0:T(8,128)(2,1)S(1)}, u32[]{:S(2)}, u32[]{:S(2)}) collective-permute-start(bf16[256,256]{1,0:T(8,128)(2,1)} %get-tuple-element.36), channel_id=1, source_target_pairs={{0,2},{1,3},{2,4},{3,5},{4,6},{5,7},{6,0},{7,1},{8,10},{9,11},{10,... | collective-permute-start | bytes 393224 | tf_op jit(solution)/shard_map/ppermute | solution.py:387

commit v3 on v2

--- a/solution.py
+++ b/solution.py
@@ -58,7 +58,7 @@
     outs = refs[: len(entries)]
     del refs[: len(entries)]
     if heading:
-        raw_scalars, scalars, kq_near = refs[:3]
+        raw_scalars, scalars, kq_near, staged, lines = refs[:5]
     sems = refs[-1]
     rows = x_ref.shape[0]
     owned = HEADS * HEAD_DIM // peers
@@ -97,16 +97,26 @@
         for p, field in enumerate(fields):
             for owner in range(peers):
                 scalars[p, owner] = field[owner * heads : (owner + 1) * heads]
+        lines[...] = jnp.zeros_like(lines)
         for i, owner in enumerate(owners):
-            outs[i][rows:] = jnp.zeros((scalar_rows, outs[i].shape[1]), jnp.bfloat16)
             for p, head, count, top, left in scalar_units(heads, rows, lead):
-                outs[i][rows + top : rows + top + count, left : left + rows] = scalars[
+                lines[i, top : top + count, left : left + rows] = scalars[
                     p, owner, head : head + count
                 ].astype(jnp.bfloat16)
             for j in range(2):
                 column = pl.multiple_of((j * GROUPS + owner // span) * STATE, LANES)
-                left = widths[0] + j * STATE
-                outs[i][0:rows, left : left + STATE] = kq_near[:, pl.ds(column, STATE)]
+                staged[i, :, j * STATE : (j + 1) * STATE] = kq_near[:, pl.ds(column, STATE)]
+            late = [
+                pltpu.make_async_copy(
+                    staged.at[i], outs[i].at[0:rows, widths[0] : lead], sems.at[3, i]
+                ),
+                pltpu.make_async_copy(
+                    lines.at[i], outs[i].at[rows : rows + scalar_rows, 0:lead], sems.at[4, i]
+                ),
+            ]
+            for copy in late:
+                copy.start()
+            copies += late
     for copy in copies:
         copy.wait()
 
@@ -357,7 +367,9 @@
             scratch.append(pltpu.VMEM((2, rows, HEADS), jnp.float32))
             scratch.append(pltpu.VMEM((FIELDS, peers, heads, rows), jnp.float32))
             scratch.append(pltpu.VMEM(key_query.shape, jnp.bfloat16))
-        scratch.append(pltpu.SemaphoreType.DMA((3, max(3, len(entries)))))
+            scratch.append(pltpu.VMEM((len(entries), rows, 2 * STATE), jnp.bfloat16))
+            scratch.append(pltpu.VMEM((len(entries), scalar_rows, lead_cols), jnp.bfloat16))
+        scratch.append(pltpu.SemaphoreType.DMA((5, max(3, len(entries)))))
         return pl.pallas_call(
             functools.partial(
                 pack_kernel,
@@ -369,7 +381,7 @@
                 scalar_rows if heading else 0,
             ),
             in_specs=in_specs,
-            out_specs=[vmem] * len(entries),
+            out_specs=[hbm] * len(entries),
             out_shape=shapes,
             scratch_shapes=scratch,
             compiler_params=pltpu.CompilerParams(vmem_limit_bytes=PACK_VMEM),
@@ -388,16 +400,16 @@
 
     far = sorted(range(2, peers - 1), key=lambda code: abs(code - peers // 2))
     near = [1, peers - 1]
-    lead = {}
-    for code, message in zip(far, pack([(code, "lead") for code in far])):
-        lead[code] = send(message, code)
-    *packed, lead[0] = pack([(code, "full") for code in near] + [(0, "full")], lead[far[0]])
-    for code, message in zip(near, packed):
-        lead[code] = send(message, code)
+    kinds = [(code, "lead") for code in far] + [(code, "full") for code in near + [0]]
+    lead = {code: message for (code, _), message in zip(kinds, pack(kinds))}
     rest = {code: lead[code] for code in near + [0]}
-    packed = pack([(code, "rest") for code in far], lead[far[0]])
-    for code, message in zip(far, packed):
-        rest[code] = send(message, code, lead[code])
+    rest.update(zip(far, pack([(code, "rest") for code in far])))
+    for code in far + near:
+        lead[code] = send(lead[code], code)
+    for code in far:
+        rest[code] = send(rest[code], code, lead[code])
+    for code in near:
+        rest[code] = lead[code]
     received = [[slots[code] for code in range(peers)] for slots in (lead, rest)]
 
     taps_x = columns(conv_inputs, me * owned, owned)

time: 139 us -> 240 us (1.73); the launches traced: 138 us -> 236 us
  Pallas kernels: 33.1 us -> 154 us
  waiting for transfers between devices: 75.8 us -> 44.8 us
  starting transfers between devices: 26.9 us -> 35.1 us
    pallas_call x3 -> x2, Pallas kernels: 8.94 us -> 130 us  [pack(): pl.pallas_call(functools.partial(pack_kernel, peers, span, widths, heads,...]
    ppermute x12, waiting for transfers between devices: 75.8 us -> 44.8 us  [send(): return lax.ppermute(message, 'ctx', pairs)]
    ppermute x12, starting transfers between devices: 26.9 us -> 35.1 us  [send(): return lax.ppermute(message, 'ctx', pairs)]
  transfers between devices with their start and end apart: 12 -> 12, of which waited for: 3 -> 4; matrix products, arithmetic and copies ran while one was open for 1% -> 1% of each run, Pallas kernels for 16% -> 16%
where the time goes in v3:
time: 240 us; the launch traced here: 236 us
  Pallas kernels  154 us (64%)
  waiting for transfers between devices  44.8 us (19%)
  starting transfers between devices  35.1 us (15%)
    pallas_call x2, Pallas kernels, pack(): pl.pallas_call(functools.partial(pack_kernel, peers, span, widths, heads,...  130 us
    ppermute x12, waiting for transfers between devices, send(): return lax.ppermute(message, 'ctx', pairs)  44.8 us
    ppermute x12, starting transfers between devices, send(): return lax.ppermute(message, 'ctx', pairs)  35.1 us
    pallas_call x2, Pallas kernels, per_device(): pl.pallas_call(functools.partial(mixer_kernel, peers, rows, heads, chunk,...  24.2 us
  transfers between devices with their start and end apart: 12, of which 4 were waited for; matrix products, arithmetic and copies ran while one was open for 1% of the time, Pallas kernels for 16%

profile of v3, /device:TPU:12, one launch (start us, length us, event | category | flops | bytes accessed | tf_op | source)
XLA Modules:
  0.0 235.7 jit_solution(7354180764796541920)
XLA Ops:
  0.0 0.0 copy-start
  0.0 0.0 copy-start.2
  0.0 108.7 %pack.2 = (bf16[264,1024]{1,0:T(8,128)(2,1)}, bf16[264,1024]{1,0:T(8,128)(2,1)}, bf16[264,1024]{1,0:T(8,128)(2,1)}, bf16[264,1024]{1,0:T(8,128)(2,1)}, bf16[264,...) custom-call(s32[1]{0:T(128)} %bitcast.refs_0_, ...), custom_call_target="tpu_custom_call" | custom-call | bytes 9461760 | tf_op jit(solution)/shard_map/pack/pallas_call | solution.py:373
  108.7 0.0 copy-start.1
  108.7 1.6 collective-permute-start.1
  110.3 0.7 collective-permute-start.3
  111.1 0.6 collective-permute-start
  111.7 1.4 collective-permute-start.11
  113.1 1.0 collective-permute-start.5
  114.1 11.2 %collective-permute-done.1.refs_3_ = bf16[264,1024]{1,0:T(8,128)(2,1)S(1)} collective-permute-done((bf16[264,1024]{1,0:T(8,128)(2,1)}, bf16[264,1024]{1,0:T(8,128)(2,1)S(1)}, u32[]{:S(2)}, u32[]{:S(2)}) %collective-permute-start.1) | collective-permute-done | bytes 540704 | tf_op jit(solution)/shard_map/ppermute | solution.py:399
  125.2 0.0 collective-permute-start.7
  125.2 20.9 %collective-permute-done.3.refs_4_ = bf16[264,1024]{1,0:T(8,128)(2,1)S(1)} collective-permute-done((bf16[264,1024]{1,0:T(8,128)(2,1)}, bf16[264,1024]{1,0:T(8,128)(2,1)S(1)}, u32[]{:S(2)}, u32[]{:S(2)}) %collective-permute-start.3) | collective-permute-done | bytes 540704 | tf_op jit(solution)/shard_map/ppermute | solution.py:399
  146.1 24.2 %collective-permute-start.9 = (bf16[264,1024]{1,0:T(8,128)(2,1)}, bf16[264,1024]{1,0:T(8,128)(2,1)}, u32[]{:S(2)}, u32[]{:S(2)}) collective-permute-start(bf16[264,1024]{1,0:T(8,128)(2,1)} %get-tuple-element.44), channel_id=1, source_target_pairs={{0,6},{1,7},{2,0},{3,1},{4,2},{5,3},{6,4},{7,5},{8,14},{9,15},{10,... | collective-permute-start | bytes 1622024 | tf_op jit(solution)/shard_map/ppermute | solution.py:399
  170.4 0.0 copy-done.2
  170.4 0.1 dynamic_slice.16
  170.4 0.1 broadcast_in_dim.4
  170.5 0.1 broadcast_in_dim_reshape.3
  170.6 21.2 %pack.3 = (bf16[256,256]{1,0:T(8,128)(2,1)}, bf16[256,256]{1,0:T(8,128)(2,1)}, bf16[256,256]{1,0:T(8,128)(2,1)}, bf16[256,256]{1,0:T(8,128)(2,1)}, bf16[256,256]{1,0:T(8,128)(2,1)}) custom-call(s32[1]{0:T(128)} %bitcast.refs_0_, bf16[256,8192]{1,0:T(8,128)(2,1)} %refs_1_.3), custom_call_target="tpu_custom_call" | custom-call | bytes 1310720 | tf_op jit(solution)/shard_map/pack/pallas_call | solution.py:373
  191.8 0.7 dynamic-slice.3
  192.5 0.0 copy-done
  192.5 0.7 constant_dynamic-slice_fusion.2
  193.2 1.1 collective-permute-done.5.refs_5_
  194.3 0.0 collective-permute-start.2
  194.3 11.6 %collective-permute-done.7.refs_6_ = bf16[264,1024]{1,0:T(8,128)(2,1)} collective-permute-done((bf16[264,1024]{1,0:T(8,128)(2,1)}, bf16[264,1024]{1,0:T(8,128)(2,1)}, u32[]{:S(2)}, u32[]{:S(2)}) %collective-permute-start.7) | collective-permute-done | bytes 540704 | tf_op jit(solution)/shard_map/ppermute | solution.py:399
  205.9 3.7 %collective-permute-start.4 = (bf16[256,256]{1,0:T(8,128)(2,1)}, bf16[256,256]{1,0:T(8,128)(2,1)S(1)}, u32[]{:S(2)}, u32[]{:S(2)}) collective-permute-start(bf16[256,256]{1,0:T(8,128)(2,1)} %get-tuple-element.36), channel_id=1, source_target_pairs={{0,3},{1,4},{2,5},{3,6},{4,7},{5,0},{6,1},{7,2},{8,11},{9,12},{10,... | collective-permute-start | bytes 393224 | tf_op jit(solution)/shard_map/ppermute | solution.py:399
  209.6 0.0 collective-permute-done.9.refs_7_
  209.6 0.7 collective-permute-start.6
  210.4 0.0 collective-permute-done.refs_2_
  210.4 0.0 collective-permute-start.8
  210.4 0.0 collective-permute-done.11.refs_8_
  210.4 1.1 collective-permute-start.10
  211.5 0.0 copy-done.1
  211.5 16.9 %mixer0.1 = (bf16[2048,768]{1,0:T(8,128)(2,1)S(1)}, f32[2048,128]{1,0:T(8,128)S(1)}, bf16[2048,256]{1,0:T(8,128)(2,1)S(1)}, bf16[2048,128]{1,0:T(8,128)(2,1)S(1)...) custom-call(s32[1]{0:T(128)} %bitcast.refs_0_, bf16[264,1280]{1,0:T(8,128)(2,1)S(1)} %copy-done.1, ...), custom_call_target="tpu_custom_call" | custom-call | flops 1415577600 | bytes 16777216 | tf_op jit(solution)/shard_map/mixer0/pallas_call | solution.py:470
  228.4 0.0 collective-permute-done.2.refs_3_
  228.4 0.0 collective-permute-done.4.refs_4_
  228.4 0.0 collective-permute-done.6.refs_5_
  228.4 0.0 collective-permute-done.8.refs_6_
  228.4 0.0 collective-permute-done.10.refs_7_
  228.4 7.3 %mixer1.1 = bf16[2048,1024]{1,0:T(8,128)(2,1)} custom-call(s32[1]{0:T(128)} %bitcast.refs_0_, bf16[264,1280]{1,0:T(8,128)(2,1)S(1)} %copy-done.1, bf16[264,1280]{1,0:T(8,128)(2,1)S(1)} %collective-permute-done.refs_2_, bf16[256,256]{1,0:T(8,128)(2,1)S(1)} %collective-permute-done.2.refs_3_, bf16[256,256]{1,0:T(8,128)(2,1)S(1)} %collective-permute-done.4.refs_4_, ...), custom_call_target="tpu_custom_call" | custom-call | flops 471859200 | bytes 5242880 | tf_op jit(solution)/shard_map/mixer1/pallas_call | solution.py:470
  (5 shorter events, 0.0 us)
Async XLA Ops:
  0.0 192.5 %copy-start = (f32[4,8192]{1,0:T(4,128)S(1)}, f32[4,8192]{1,0:T(4,128)}, u32[]{:S(2)}) copy-start(f32[4,8192]{1,0:T(4,128)} %param.10) | copy-start | bytes 393220
  0.0 170.4 %copy-start.2 = (f32[128]{0:T(128)S(1)}, f32[128]{0:T(128)}, u32[]{:S(2)}) copy-start(f32[128]{0:T(128)} %param.14) | copy-start | bytes 1540
  108.7 102.8 %copy-start.1 = (bf16[264,1280]{1,0:T(8,128)(2,1)S(1)}, bf16[264,1280]{1,0:T(8,128)(2,1)}, u32[]{:S(2)}) copy-start(bf16[264,1280]{1,0:T(8,128)(2,1)} %get-tuple-element.29.refs_1_) | copy-start | bytes 2027524
  108.7 16.5 %collective-permute-start.1 = (bf16[264,1024]{1,0:T(8,128)(2,1)}, bf16[264,1024]{1,0:T(8,128)(2,1)S(1)}, u32[]{:S(2)}, u32[]{:S(2)}) collective-permute-start(bf16[264,1024]{1,0:T(8,128)(2,1)} %get-tuple-element.32), channel_id=1, source_target_pairs={{0,2},{1,3},{2,4},{3,5},{4,6},{5,7},{6,0},{7,1},{8,10},{9,11},{10,... | collective-permute-start | bytes 1622024 | tf_op jit(solution)/shard_map/ppermute | solution.py:399
  110.3 35.8 %collective-permute-start.3 = (bf16[264,1024]{1,0:T(8,128)(2,1)}, bf16[264,1024]{1,0:T(8,128)(2,1)S(1)}, u32[]{:S(2)}, u32[]{:S(2)}) collective-permute-start(bf16[264,1024]{1,0:T(8,128)(2,1)} %get-tuple-element.35), channel_id=1, source_target_pairs={{0,3},{1,4},{2,5},{3,6},{4,7},{5,0},{6,1},{7,2},{8,11},{9,12},{10,... | collective-permute-start | bytes 1622024 | tf_op jit(solution)/shard_map/ppermute | solution.py:399
  111.1 99.3 %collective-permute-start = (bf16[264,1280]{1,0:T(8,128)(2,1)}, bf16[264,1280]{1,0:T(8,128)(2,1)S(1)}, u32[]{:S(2)}, u32[]{:S(2)}) collective-permute-start(bf16[264,1280]{1,0:T(8,128)(2,1)} %get-tuple-element.30), channel_id=1, source_target_pairs={{0,1},{1,2},{2,3},{3,4},{4,5},{5,6},{6,7},{7,0},{8,9},{9,10},{10,1... | collective-permute-start | bytes 2027528 | tf_op jit(solution)/shard_map/ppermute | solution.py:399
  111.7 98.7 %collective-permute-start.11 = (bf16[264,1280]{1,0:T(8,128)(2,1)}, bf16[264,1280]{1,0:T(8,128)(2,1)S(1)}, u32[]{:S(2)}, u32[]{:S(2)}) collective-permute-start(bf16[264,1280]{1,0:T(8,128)(2,1)} %get-tuple-element.46), channel_id=1, source_target_pairs={{0,7},{1,0},{2,1},{3,2},{4,3},{5,4},{6,5},{7,6},{8,15},{9,8},{10,9... | collective-permute-start | bytes 2027528 | tf_op jit(solution)/shard_map/ppermute | solution.py:399
  113.1 81.2 %collective-permute-start.5 = (bf16[264,1024]{1,0:T(8,128)(2,1)}, bf16[264,1024]{1,0:T(8,128)(2,1)}, u32[]{:S(2)}, u32[]{:S(2)}) collective-permute-start(bf16[264,1024]{1,0:T(8,128)(2,1)} %get-tuple-element.38), channel_id=1, source_target_pairs={{0,4},{1,5},{2,6},{3,7},{4,0},{5,1},{6,2},{7,3},{8,12},{9,13},{10,... | collective-permute-start | bytes 1622024 | tf_op jit(solution)/shard_map/ppermute | solution.py:399
  125.2 80.7 %collective-permute-start.7 = (bf16[264,1024]{1,0:T(8,128)(2,1)}, bf16[264,1024]{1,0:T(8,128)(2,1)}, u32[]{:S(2)}, u32[]{:S(2)}) collective-permute-start(bf16[264,1024]{1,0:T(8,128)(2,1)} %get-tuple-element.41), channel_id=1, source_target_pairs={{0,5},{1,6},{2,7},{3,0},{4,1},{5,2},{6,3},{7,4},{8,13},{9,14},{10,... | collective-permute-start | bytes 1622024 | tf_op jit(solution)/shard_map/ppermute | solution.py:399
  146.1 63.5 %collective-permute-start.9 = (bf16[264,1024]{1,0:T(8,128)(2,1)}, bf16[264,1024]{1,0:T(8,128)(2,1)}, u32[]{:S(2)}, u32[]{:S(2)}) collective-permute-start(bf16[264,1024]{1,0:T(8,128)(2,1)} %get-tuple-element.44), channel_id=1, source_target_pairs={{0,6},{1,7},{2,0},{3,1},{4,2},{5,3},{6,4},{7,5},{8,14},{9,15},{10,... | collective-permute-start | bytes 1622024 | tf_op jit(solution)/shard_map/ppermute | solution.py:399
  194.3 34.1 %collective-permute-start.2 = (bf16[256,256]{1,0:T(8,128)(2,1)}, bf16[256,256]{1,0:T(8,128)(2,1)S(1)}, u32[]{:S(2)}, u32[]{:S(2)}) collective-permute-start(bf16[256,256]{1,0:T(8,128)(2,1)} %get-tuple-element.33), channel_id=1, source_target_pairs={{0,2},{1,3},{2,4},{3,5},{4,6},{5,7},{6,0},{7,1},{8,10},{9,11},{10,... | collective-permute-start | bytes 393224 | tf_op jit(solution)/shard_map/ppermute | solution.py:399
  205.9 22.5 %collective-permute-start.4 = (bf16[256,256]{1,0:T(8,128)(2,1)}, bf16[256,256]{1,0:T(8,128)(2,1)S(1)}, u32[]{:S(2)}, u32[]{:S(2)}) collective-permute-start(bf16[256,256]{1,0:T(8,128)(2,1)} %get-tuple-element.36), channel_id=1, source_target_pairs={{0,3},{1,4},{2,5},{3,6},{4,7},{5,0},{6,1},{7,2},{8,11},{9,12},{10,... | collective-permute-start | bytes 393224 | tf_op jit(solution)/shard_map/ppermute | solution.py:399
  209.6 18.8 %collective-permute-start.6 = (bf16[256,256]{1,0:T(8,128)(2,1)}, bf16[256,256]{1,0:T(8,128)(2,1)S(1)}, u32[]{:S(2)}, u32[]{:S(2)}) collective-permute-start(bf16[256,256]{1,0:T(8,128)(2,1)} %get-tuple-element.39), channel_id=1, source_target_pairs={{0,4},{1,5},{2,6},{3,7},{4,0},{5,1},{6,2},{7,3},{8,12},{9,13},{10,... | collective-permute-start | bytes 393224 | tf_op jit(solution)/shard_map/ppermute | solution.py:399
  210.4 18.0 %collective-permute-start.8 = (bf16[256,256]{1,0:T(8,128)(2,1)}, bf16[256,256]{1,0:T(8,128)(2,1)S(1)}, u32[]{:S(2)}, u32[]{:S(2)}) collective-permute-start(bf16[256,256]{1,0:T(8,128)(2,1)} %get-tuple-element.42), channel_id=1, source_target_pairs={{0,5},{1,6},{2,7},{3,0},{4,1},{5,2},{6,3},{7,4},{8,13},{9,14},{10,... | collective-permute-start | bytes 393224 | tf_op jit(solution)/shard_map/ppermute | solution.py:399
  210.4 18.0 %collective-permute-start.10 = (bf16[256,256]{1,0:T(8,128)(2,1)}, bf16[256,256]{1,0:T(8,128)(2,1)S(1)}, u32[]{:S(2)}, u32[]{:S(2)}) collective-permute-start(bf16[256,256]{1,0:T(8,128)(2,1)} %get-tuple-element.45), channel_id=1, source_target_pairs={{0,6},{1,7},{2,0},{3,1},{4,2},{5,3},{6,4},{7,5},{8,14},{9,15},{10,... | collective-permute-start | bytes 393224 | tf_op jit(solution)/shard_map/ppermute | solution.py:399
